TPU v7x, 32 devices: a whole 2x2x4 slice. The times are simulated.
32 devices in a mesh: feed: 8 (over z, core), chan: 4 (over y, x).
Axes of the slice: x: 2, y: 2, z: 4, core: 2. Of those that a mesh axis runs over, the one named last changes fastest.
Arguments:
- raw_samples: bfloat16 [256, 90112], P(('feed', 'chan')), may hold values from -6 to 6
- stack_code: int32 [256, 256], P('feed'), may hold values from -382 to 381, as said below
- stack_owner: int32 [382], replicated, may hold values from 0 to 7, as said below
Outputs:
- visibilities: float32 [760, 2, 2048], P('feed', None, 'chan')
Inputs may be any that keep to these rules, and one draw needn't show every extreme that they name: `stack_code`: entry [i, j] names the stack of the baseline from input i to input j: s when it has stack s's orientation, -1 - s when reversed. For i != j entry [j, i] is -1 minus entry [i, j]; the diagonal holds 0; every stack is named. `stack_owner`: no owner has more than 95 stacks, and one owner has exactly 95.
All inputs are finite; a program needn't handle non-finite values.
Results may differ from a plain program's by a relative error of at most 0.0083.
Values may be sent and summed in bfloat16 or wider, within the bound.
No kernel may reach another device: no remote copies, remote signals or barrier semaphores. Data moves between devices by JAX's collectives and lax.ppermute only.
A program may use at most 128 MiB of HBM per device.

v0:
```python
import math

import jax
import jax.numpy as jnp
from jax import lax
from jax.sharding import PartitionSpec as P

SPECTRA = 4
TAPS = 8
FA = 64
FB = 128
FRAME = 8192
CHANS = 2048
STACKS = 382


def window_table():
    length = TAPS * FRAME
    sample = jnp.arange(length).astype(jnp.float32)
    centred = (sample - length / 2 + 0.5) / FRAME
    hanning = 0.5 - 0.5 * jnp.cos(2.0 * math.pi * (sample + 0.5) / length)
    weights = jnp.sinc(centred) * hanning
    weights = weights * jnp.sqrt(FRAME / jnp.sum(weights * weights))
    return weights.reshape(TAPS, FRAME)


def angle_of(left_index, right_index, modulus):
    product = left_index[:, None] * right_index[None, :] % modulus
    return 2.0 * math.pi * product.astype(jnp.float32) / modulus


def first_table():
    angles = angle_of(jnp.arange(FA, dtype=jnp.int32), jnp.arange(FA, dtype=jnp.int32), FA)
    return jnp.concatenate([jnp.cos(angles), -jnp.sin(angles)], axis=1).astype(jnp.bfloat16)


def twiddles():
    angles = angle_of(jnp.arange(FA, dtype=jnp.int32), jnp.arange(FB, dtype=jnp.int32), FRAME)
    return (jnp.cos(angles), jnp.sin(angles))


def second_table(second_count):
    angles = angle_of(
        jnp.arange(FB, dtype=jnp.int32), jnp.arange(second_count, dtype=jnp.int32), FB
    )
    cosine = jnp.cos(angles)
    sine_part = jnp.sin(angles)
    top_rows = jnp.stack([cosine, -sine_part], axis=1)
    low_rows = jnp.stack([sine_part, cosine], axis=1)
    return jnp.stack([top_rows, low_rows], axis=0).astype(jnp.bfloat16)


def channelize(samples, second_count):
    window = window_table()
    inputs = samples.shape[0]
    framed = samples.reshape(inputs, SPECTRA + TAPS - 1, FRAME)
    summed = jnp.zeros((inputs, SPECTRA, FRAME), jnp.float32)
    for tap_index in range(TAPS):
        summed = summed + window[tap_index] * framed[:, tap_index : tap_index + SPECTRA]
    frames = summed.astype(jnp.bfloat16).reshape(inputs * SPECTRA, FA, FB)
    sectioned = jnp.einsum("rab,ak->rkb", frames, first_table(), preferred_element_type=jnp.float32)
    cosine, sine_part = twiddles()
    real_part = sectioned[:, :FA]
    imag_part = sectioned[:, FA:]
    mixed = jnp.stack(
        [real_part * cosine + imag_part * sine_part, imag_part * cosine - real_part * sine_part],
        axis=2,
    )
    mixed = mixed.astype(jnp.bfloat16)
    spectra = jnp.einsum(
        "rkpb,pbqm->rqmk", mixed, second_table(second_count), preferred_element_type=jnp.float32
    )
    spectra = spectra / math.sqrt(FRAME)
    return spectra.reshape(inputs, SPECTRA, 2, second_count * FA).astype(jnp.bfloat16)


def correlate(own_block, other_block):
    left_rows = own_block.reshape(own_block.shape[0], 2 * own_block.shape[1], own_block.shape[3])
    turned = jnp.stack([-other_block[:, :, 1], other_block[:, :, 0]], axis=2)
    right_rows = jnp.stack([other_block, turned], axis=3)
    right_rows = right_rows.reshape(
        other_block.shape[0], 2 * other_block.shape[1], 2, other_block.shape[3]
    )
    return jnp.einsum("ikc,jkqc->ijqc", left_rows, right_rows, preferred_element_type=jnp.float32)


def stack_targets(code_rows, usable):
    target = jnp.where(code_rows >= 0, code_rows, -1 - code_rows)
    return jnp.where(usable, target, STACKS)


def oriented(values, code_rows):
    orient = jnp.where(code_rows >= 0, 1.0, -1.0).astype(jnp.float32)
    return jnp.stack([values[:, :, 0], values[:, :, 1] * orient[:, :, None]], axis=2)


def stack_dense(values, code_rows, usable):
    target = stack_targets(code_rows, usable).reshape(-1)
    values = oriented(values, code_rows)
    width = values.shape[3]
    flattened = values.reshape(-1, 2 * width)
    member = (target[:, None] == jnp.arange(STACKS + 1, dtype=jnp.int32)[None, :]).astype(
        jnp.float32
    )
    summed = lax.dot_general(
        member,
        flattened,
        (((0,), (0,)), ((), ())),
        precision=lax.Precision.HIGHEST,
        preferred_element_type=jnp.float32,
    )
    return summed.reshape(STACKS + 1, 2, width)


def slot_sources(owner_ids, owners, capacity, stacks):
    member = (owner_ids[:, None] == jnp.arange(owners, dtype=jnp.int32)[None, :]).astype(jnp.int32)
    earlier = jnp.cumsum(member, axis=0) - member
    ranking = jnp.sum(earlier * member, axis=1)
    slot_ids = owner_ids * capacity + ranking
    filled = jnp.full((owners * capacity,), stacks, jnp.int32)
    return filled.at[slot_ids].set(jnp.arange(stacks, dtype=jnp.int32))


def per_device(raw_samples, stack_code, stack_owner):
    local_spectra = channelize(raw_samples, CHANS // FA)
    own_block = lax.all_to_all(local_spectra, "chan", split_axis=3, concat_axis=0, tiled=True)
    height = own_block.shape[0]
    feeds = lax.axis_size("feed")
    myself = lax.axis_index("feed")
    capacity = 2 * STACKS // feeds
    sources = slot_sources(stack_owner, feeds, capacity, STACKS)
    row_ids = myself * height + jnp.arange(height, dtype=jnp.int32)
    pieces = lax.all_gather(own_block, "feed", axis=0, tiled=True)
    col_ids = jnp.arange(pieces.shape[0], dtype=jnp.int32)
    usable = col_ids[None, :] > row_ids[:, None]
    totals = stack_dense(correlate(own_block, pieces), stack_code, usable)
    all_cols = jnp.arange(stack_code.shape[1], dtype=jnp.int32)
    upper = all_cols[None, :] > row_ids[:, None]
    target = stack_targets(stack_code, upper)
    counts = jax.ops.segment_sum(
        jnp.ones((target.size,), jnp.float32), target.reshape(-1), num_segments=STACKS + 1
    )
    cleaned = totals.at[STACKS].set(0.0)
    weights = counts.at[STACKS].set(0.0)
    summed, tallies = (
        lax.psum_scatter(cleaned[sources], "feed", scatter_dimension=0, tiled=True),
        lax.psum_scatter(weights[sources], "feed", scatter_dimension=0, tiled=True),
    )
    return summed / jnp.maximum(tallies, 1.0)[:, None, None]


def solution(mesh):
    placed = (P(("feed", "chan"), None), P("feed", None), P())
    return jax.shard_map(
        per_device, mesh=mesh, in_specs=placed, out_specs=P("feed", None, "chan"), check_vma=False
    )
```

profile of v0, /device:TPU:0, one launch (start us, length us, event | category | flops | bytes accessed | tf_op | source)
XLA Modules:
  0.0 322.2 jit_solution(4269579584987717627)
XLA Ops:
  6.5 0.0 all-gather.2.cloned.1.call-start
  6.5 1.8 multiply_reduce_fusion
  8.4 0.2 negate_convert_fusion
  8.5 0.1 fusion.48
  8.7 0.1 negate_convert_fusion.1
  8.8 0.1 fusion.56
  9.6 1.2 broadcast_multiply_fusion
  10.8 3.3 %add_convert_fusion.1 = bf16[8,4,8192]{2,0,1:T(8,128)(2,1)S(1)} fusion(bf16[8,11,8192]{2,0,1:T(8,128)(2,1)} %bitcast.83, f32[8192]{0:T(1024)S(1)} %get-tuple-element.38, f32[8192]{0:T(1024)S(1)} %get-tuple-element.39, f32[8192]{0:T(1024)S(1)} %get-tuple-element.40, f32[8192]{0:T(1024)S(1)} %get-tuple-element.41, f32[8192]{0:T(1024)S(1)} %get-tuple-element.42, ...), kind=kLoop, calls=%fused_computation.26 | loop fusion | flops 6291456 | bytes 4980736 | tf_op jit(solution)/shard_map/convert_element_type | solution.py:60
  14.2 0.4 copy.29
  14.6 0.5 reshape.226
  15.1 0.5 convolution_bitcast_fusion.1
  15.6 0.3 fusion.12
  16.0 0.6 fusion.9
  16.6 0.4 convert_element_type.114
  17.0 7.4 %copy.31 = bf16[8,4,2,2048]{0,2,1,3:T(2,128)(2,1)} copy(bf16[8,4,2,2048]{3,1,0,2:T(4,128)(2,1)S(1)} %convert_element_type.114) | data formatting | bytes 524288 | tf_op jit(solution)/shard_map/convert_element_type | solution.py:74
  24.4 5.8 %reshape.281 = bf16[4,2,16384]{2,1,0:T(2,128)(2,1)S(1)} reshape(bf16[2048,4,2,8]{3,2,1,0:T(2,128)(2,1)} %bitcast.81) | data formatting | bytes 524288
  30.1 10.7 %all_to_all.18 = bf16[4,2,16384]{2,1,0:T(2,128)(2,1)S(1)} all-to-all(bf16[4,2,16384]{2,1,0:T(2,128)(2,1)S(1)} %reshape.281), channel_id=1, replica_groups=mesh['feed'=8,'chan'=4] {'chan'}, dimensions={0} | all-to-all | bytes 524288 | tf_op jit(solution)/shard_map/all_to_all | solution.py:126
  40.8 5.9 %reshape.282 = bf16[2048,4,2,8]{3,2,1,0:T(2,128)(2,1)} reshape(bf16[4,2,16384]{2,1,0:T(2,128)(2,1)S(1)} %all_to_all.18) | data formatting | bytes 524288
  46.7 0.0 copy-start
  46.7 0.0 copy-start.1
  46.7 9.5 %copy.43 = bf16[8,4,2,4,512]{4,3,0,2,1:T(4,128)(2,1)S(1)} copy(bf16[8,4,2,4,512]{0,2,1,4,3:T(2,128)(2,1)} %bitcast.82) | data formatting | bytes 524288 | tf_op jit(solution)/shard_map/all_to_all | solution.py:126
  56.3 0.8 copy.56
  57.0 0.0 all-gather.2.cloned.1.call-update
  57.1 0.0 all-reduce.5.cloned.1.call-start
  57.1 0.0 copy-done
  57.1 0.1 fusion.28
  57.2 0.0 copy-done.1
  57.3 0.9 reduce-window.6
  58.1 0.2 slice_reduce_fusion
  58.4 0.1 add_bitcast_fusion
  58.5 3.1 scatter_custom_fusion
  61.7 1.7 copy.42
  63.4 22.6 %all-gather.2.cloned.1.call-done = bf16[256,4,2,512]{3,0,2,1:T(8,128)(2,1)} async-done(((bf16[32,4,2,512]{3,0,2,1:T(8,128)(2,1)}), bf16[256,4,2,512]{3,0,2,1:T(8,128)(2,1)}) %all-gather.2.cloned.1.call-update) | async-done | bytes 2097168 | tf_op jit(solution)/shard_map/all_gather | solution.py:133
  86.0 1.7 slice_negate_fusion
  87.7 1.5 pad_maximum_fusion.1
  89.2 3.3 %copy.45 = bf16[256,8,1,512]{0,1,2,3:T(8,128)(2,1)S(1)} copy(bf16[256,8,1,512]{3,0,1,2:T(8,128)(2,1)} %bitcast.85) | data formatting | bytes 4194304 | tf_op jit(solution)/shard_map/stack | solution.py:80
  92.5 4.5 %copy.44 = bf16[256,8,1,512]{0,1,2,3:T(8,128)(2,1)} copy(bf16[256,8,1,512]{3,0,1,2:T(8,128)(2,1)} %bitcast.84) | data formatting | bytes 4194304 | tf_op jit(solution)/shard_map/stack | solution.py:80
  97.0 17.2 %convolution_bitcast_fusion = f32[32,256,2,512]{1,0,2,3:T(8,128)} fusion(bf16[32,8,512,1]{0,1,3,2:T(8,128)(2,1)S(1)} %copy.42, bf16[256,8,1,512]{0,1,2,3:T(8,128)(2,1)S(1)} %copy.45, bf16[256,8,1,512]{0,1,2,3:T(8,128)(2,1)} %copy.44), kind=kOutput, calls=%fused_computation.6 | convolution fusion | flops 136314880 | bytes 38010880 | tf_op jit(solution)/shard_map/ikc,jkqc->ijqc/dot_general | solution.py:84
  114.2 22.1 %fusion.64 = (f32[32,256,1,512]{1,0,2,3:T(8,128)}, f32[32,256,1,512]{1,0,2,3:T(8,128)}) fusion(f32[32,256,2,512]{1,0,2,3:T(8,128)} %convolution_bitcast_fusion, f32[32,256]{1,0:T(8,128)S(1)} %compare_select_fusion), kind=kLoop, calls=%fused_computation.126 | loop fusion | flops 4194304 | bytes 67141632 | tf_op jit(solution)/shard_map/slice | solution.py:94
  136.3 12.2 %pad_maximum_fusion = f32[32,256,2,512]{1,0,2,3:T(8,128)S(1)} fusion(f32[32,256,1,512]{1,0,2,3:T(8,128)} %get-tuple-element.30, f32[32,256,1,512]{1,0,2,3:T(8,128)} %get-tuple-element.29), kind=kLoop, calls=%fused_computation.4 | loop fusion | flops 8388608 | bytes 67108864 | tf_op jit(solution)/shard_map/stack | solution.py:94
  148.5 11.1 %copy.38 = f32[32,256,2,512]{1,0,3,2:T(8,128)} copy(f32[32,256,2,512]{1,0,2,3:T(8,128)S(1)} %pad_maximum_fusion) | data formatting | bytes 67108864 | tf_op jit(solution)/shard_map/stack | solution.py:94
  159.6 36.3 %copy.49 = f32[128,8,32,256]{3,1,2,0:T(8,128)} copy(f32[128,8,32,256]{3,2,1,0:T(8,128)} %bitcast.79) | data formatting | bytes 67108864
  195.9 31.4 %fusion.1 = f32[383,2,512]{2,0,1:T(8,128)S(1)} fusion(f32[2,512,8192]{2,1,0:T(8,128)} %bitcast.80, s32[8192]{0:T(1024)S(1)} %bitcast.89), kind=kOutput, calls=%fused_computation.9 | convolution fusion | flops 38557179904 | bytes 35155968 | tf_op jit(solution)/shard_map/dot_general | solution.py:105
  227.3 0.1 scatter.14
  227.4 1.2 copy.39
  228.6 5.7 %gather_fusion = f32[760,2,512]{2,1,0:T(2,128)} fusion(f32[383,2,512]{2,1,0:T(2,128)S(1)} %copy.39, s32[1024]{0:T(1024)S(1)} %pad_clamp_fusion), kind=kCustom, calls=%fused_computation | custom fusion | bytes 6228960 | tf_op jit(solution)/shard_map/gather | solution.py:146
  234.3 0.0 copy-start.2
  234.3 0.0 all-reduce.5.cloned.1.call-update
  234.3 57.0 %scatter_custom_fusion.1 = f32[383]{0:T(512)S(1)} fusion(s32[8192]{0:T(1024)S(1)} %bitcast.90, f32[8192]{0:T(1024)S(1)} %broadcast.269, f32[]{:T(128)} %constant.179.clone.1), kind=kCustom, calls=%fused_computation.117 | custom fusion | flops 8192 | bytes 1536 | tf_op jit(solution)/shard_map/scatter-add | solution.py:140
  291.4 5.0 %gather_fusion.1 = f32[760]{0:T(1024)S(1)} fusion(f32[383]{0:T(512)S(1)} %constant_dynamic-update-slice_fusion, s32[1024]{0:T(1024)S(1)} %pad_clamp_fusion), kind=kCustom, calls=%fused_computation.1 | custom fusion | bytes 9120 | tf_op jit(solution)/shard_map/gather | solution.py:147
  296.4 0.0 copy-done.2
  296.4 0.6 dynamic-slice.13
  297.6 15.7 %all-reduce.2 = f32[760]{0:T(1024)S(1)} all-reduce(f32[760]{0:T(1024)S(1)} %gather_fusion.1), channel_id=3, replica_groups=mesh['feed'=8,'chan'=4] {'feed'}, use_global_device_ids=true, to_apply=%region_7.8.clone | all-reduce | flops 760 | bytes 6080
  313.3 0.1 dynamic-slice_maximum_fusion
  313.4 0.0 all-reduce.5.cloned.1.call-done
  313.4 1.9 dynamic-slice_divide_fusion
  (16 shorter events, 0.2 us)
Async XLA Ops:
  6.5 79.5 %all-gather.2.cloned.1.call-start = ((), (), s32[]{:S(2)}) async-start(), calls=%async_computation.1 | async-start | bytes 2359296 | tf_op jit(solution)/shard_map/all_gather | solution.py:133
  46.7 10.4 %copy-start = (s32[32,256]{1,0:T(8,128)S(1)}, s32[32,256]{1,0:T(8,128)}, u32[]{:S(2)}) copy-start(s32[32,256]{1,0:T(8,128)} %param.8) | copy-start | bytes 98308
  46.7 10.5 %copy-start.1 = (s32[382]{0:T(512)S(1)}, s32[382]{0:T(512)}, u32[]{:S(2)}) copy-start(s32[382]{0:T(512)} %param.9) | copy-start | bytes 4588
  57.1 256.4 %all-reduce.5.cloned.1.call-start = ((), (), s32[]{:S(2)}) async-start(), calls=%async_computation.2 | async-start | bytes 6225920
  234.3 62.1 %copy-start.2 = (u32[32]{0:T(128)S(1)}, u32[32]{0:T(128)}, u32[]{:S(2)}) copy-start(u32[32]{0:T(128)} %constant.207) | copy-start | bytes 388
Sparse Core Ops, SparseCore 0:
  57.2 28.8 all-gather.1
  234.5 76.3 all-reduce.4
where the time goes:
time: 323 us; the launch traced here: 322 us
  other arithmetic  105 us (33%)
  local copies, waits for them, and re-layouts  104 us (32%)
  matrix products  49.7 us (15%)
  blocking collectives  26.4 us (8%)
  waiting for transfers between devices  22.7 us (7%)
  between operations  15.1 us (5%)
    scatter-add x1, other arithmetic, per_device(): jax.ops.segment_sum(jnp.ones((target.size,), jnp.float32), target.reshape...  57 us
    unnamed x11, local copies, waits for them, and re-layouts  48.6 us
    dot_general x1, matrix products, stack_dense(): lax.dot_general(member, flattened, (((0,), (0,)), ((), ())), precision=la...  31.4 us
    all_gather x1, waiting for transfers between devices, per_device(): pieces = lax.all_gather(own_block, 'feed', axis=0, tiled=True)  22.6 us
    slice x1, other arithmetic, oriented(): values[:, :, 0]  22.1 us
    dot_general x1, matrix products, correlate(): jnp.einsum('ikc,jkqc->ijqc', left_rows, right_rows, preferred_element_typ...  17.2 us
    unnamed x1, blocking collectives  15.7 us
    another operation x1, other arithmetic, oriented(): jnp.stack([values[:, :, 0], values[:, :, 1] * orient[:, :, None]], axis=2)  12.2 us
  transfers between devices with their start and end apart: 2, of which 1 were waited for; matrix products, arithmetic and copies ran while one was open for 21% of the time, Pallas kernels for 0%

commit v1 on v0

v1 whole, which is shorter than its diff:
```python
import functools
import math

import jax
import jax.numpy as jnp
import numpy as np
from jax import lax
from jax.experimental import pallas as pl
from jax.experimental.pallas import tpu as pltpu
from jax.sharding import PartitionSpec as P

SPECTRA = 4
TAPS = 8
FA = 64
FB = 128
FRAME = 8192
CHANS = 2048
STACKS = 382
QS = CHANS // FA
STACK_ROWS = 384
HALF_STACKS = 192
GROUP = 8
MB = 1024 * 1024


def window_table():
    length = TAPS * FRAME
    sample = np.arange(length, dtype=np.float64)
    centred = (sample - length / 2 + 0.5) / FRAME
    hanning = 0.5 - 0.5 * np.cos(2.0 * np.pi * (sample + 0.5) / length)
    weights = np.sinc(centred) * hanning
    weights = weights * np.sqrt(FRAME / np.sum(weights * weights))
    return weights.reshape(TAPS, FRAME).astype(np.float32)


def angle_of(left_count, right_count, modulus):
    product = np.arange(left_count)[:, None] * np.arange(right_count)[None, :] % modulus
    return 2.0 * np.pi * product / modulus


def first_table():
    angles = angle_of(FA, FA, FA)
    return np.concatenate([np.cos(angles), -np.sin(angles)], axis=0)


def twiddles():
    angles = angle_of(FA, FB, FRAME)
    return np.cos(angles).astype(np.float32), np.sin(angles).astype(np.float32)


def second_table(order):
    angles = angle_of(FB, QS, FB).T[np.asarray(order)]
    cosine, sine = np.cos(angles), np.sin(angles)
    real_rows = np.concatenate([cosine, sine], axis=1)
    imag_rows = np.concatenate([-sine, cosine], axis=1)
    return np.concatenate([real_rows, imag_rows], axis=0)


def channelize_kernel(
    x_ref, window_ref, first_ref, cos_ref, sin_ref, second_ref, out_ref, frames, mixed, turned
):
    inputs = x_ref.shape[0]
    for a in range(FA):
        sums = [None] * SPECTRA
        for r in range(SPECTRA + TAPS - 1):
            x = x_ref[:, r * FRAME + a * FB : r * FRAME + (a + 1) * FB].astype(jnp.float32)
            for t in range(SPECTRA):
                if 0 <= r - t < TAPS:
                    term = window_ref[r - t : r - t + 1, a * FB : (a + 1) * FB] * x
                    sums[t] = term if sums[t] is None else sums[t] + term
        for t in range(SPECTRA):
            frames[pl.ds(t * inputs * FA + a, inputs, stride=FA), :] = sums[t]
    for t in range(SPECTRA):
        rows = frames[t * inputs * FA : (t + 1) * inputs * FA, :].astype(jnp.bfloat16)
        wide = jnp.concatenate([rows[i * FA : (i + 1) * FA] for i in range(inputs)], axis=1)
        section = jnp.dot(first_ref[...], wide, preferred_element_type=jnp.float32)
        for i in range(inputs):
            real = section[:FA, i * FB : (i + 1) * FB]
            imag = section[FA:, i * FB : (i + 1) * FB]
            cosine, sine = cos_ref[...], sin_ref[...]
            twisted = jnp.concatenate(
                [real * cosine + imag * sine, imag * cosine - real * sine], axis=1
            ).astype(jnp.bfloat16)
            for h in range(2):
                start = ((i * 2 + h) * SPECTRA + t) * 32
                mixed[start : start + 32, :] = twisted[h * 32 : (h + 1) * 32]
    for i in range(inputs):
        spectra = lax.dot_general(
            second_ref[...],
            mixed[i * 256 : (i + 1) * 256, :],
            (((1,), (1,)), ((), ())),
            preferred_element_type=jnp.float32,
        ) * (1.0 / math.sqrt(FRAME))
        for m in range(2):
            for g in range(QS // 8):
                for h in range(2):
                    tile = spectra[m * QS + g * 8 : m * QS + g * 8 + 8, h * 128 : (h + 1) * 128]
                    start = ((h * 2 + m) * QS + g * 8) * inputs + i
                    turned[pl.ds(start, 8, stride=inputs), :] = tile
    for part in range(4):
        rows = turned[part * QS * inputs : (part + 1) * QS * inputs, :]
        out_ref[:, part * 128 : (part + 1) * 128] = rows.astype(jnp.bfloat16)


def channelize(samples, order):
    inputs = samples.shape[0]
    cosine, sine = twiddles()
    return pl.pallas_call(
        channelize_kernel,
        out_shape=jax.ShapeDtypeStruct((QS * inputs, 512), jnp.bfloat16),
        scratch_shapes=[
            pltpu.VMEM((SPECTRA * inputs * FA, FB), jnp.float32),
            pltpu.VMEM((SPECTRA * inputs * FA, 2 * FB), jnp.bfloat16),
            pltpu.VMEM((4 * QS * inputs, 128), jnp.float32),
        ],
        compiler_params=pltpu.CompilerParams(vmem_limit_bytes=32 * MB),
        name="channelize",
    )(
        samples,
        jnp.asarray(window_table()),
        jnp.asarray(first_table(), jnp.bfloat16),
        jnp.asarray(cosine),
        jnp.asarray(sine),
        jnp.asarray(second_table(order), jnp.bfloat16),
    )


def one_hot(stack, row):
    return jnp.where(stack == row, jnp.ones_like(stack), jnp.zeros_like(stack))


def stack_ids(inputs):
    ids = lax.broadcasted_iota(jnp.int32, (STACK_ROWS, inputs), 0) - HALF_STACKS
    return ids.astype(jnp.float32).astype(jnp.bfloat16)


def targets_kernel(padded, code_ref, owner_ref, target_ref, sign_ref, count_ref, slot_ref):
    inputs = code_ref.shape[1]
    half = inputs // 2
    row = lax.broadcasted_iota(jnp.int32, (half, inputs), 0)
    col = lax.broadcasted_iota(jnp.int32, (half, inputs), 1)
    apart = jnp.bitwise_and(col - row, inputs - 1)
    code = jnp.where((apart >= 1) & (apart <= half), code_ref[:half, :], code_ref[half:, :])
    target = jnp.where(code >= 0, code, -1 - code)
    target = jnp.where(apart == 0, STACK_ROWS, target) - HALF_STACKS
    target_ref[...] = target.astype(jnp.float32)
    sign_ref[...] = jnp.where(code >= 0, 1.0, -1.0)
    stack = stack_ids(inputs)
    ones = jnp.ones((GROUP * inputs, 128), jnp.bfloat16)
    count_ref[...] = jnp.zeros(count_ref.shape, jnp.float32)

    def step(g, carry):
        rows = target_ref[pl.ds(pl.multiple_of(g * GROUP, GROUP), GROUP), :].astype(jnp.bfloat16)
        member = jnp.concatenate([one_hot(stack, rows[u : u + 1]) for u in range(GROUP)], axis=1)
        count_ref[...] += jnp.dot(member, ones, preferred_element_type=jnp.float32)
        return carry

    lax.fori_loop(0, half // GROUP, step, 0)

    owner = owner_ref[...]
    across = jnp.broadcast_to(owner, (STACK_ROWS, STACK_ROWS))
    down = across.T
    before = lax.broadcasted_iota(jnp.int32, (STACK_ROWS, STACK_ROWS), 0)
    after = lax.broadcasted_iota(jnp.int32, (STACK_ROWS, STACK_ROWS), 1)
    earlier = jnp.where((across == down) & (before < after), 1.0, 0.0)
    rank = jnp.sum(earlier, axis=0, keepdims=True)
    slot_ref[...] = jnp.where(owner >= 0, owner * padded, -1.0) + rank


def targets(codes, owner, padded):
    inputs = codes.shape[1]
    return pl.pallas_call(
        functools.partial(targets_kernel, padded),
        out_shape=(
            jax.ShapeDtypeStruct((inputs // 2, inputs), jnp.float32),
            jax.ShapeDtypeStruct((inputs // 2, inputs), jnp.float32),
            jax.ShapeDtypeStruct((STACK_ROWS, 128), jnp.float32),
            jax.ShapeDtypeStruct((1, STACK_ROWS), jnp.float32),
        ),
        compiler_params=pltpu.CompilerParams(vmem_limit_bytes=32 * MB),
        name="targets",
    )(codes, owner)


def stack_kernel(
    spectra_ref, target_ref, sign_ref, count_ref, slot_ref, out_ref, wide, other, acc
):
    inputs, lanes = spectra_ref.shape
    half, blocks = inputs // 2, lanes // 256
    wide[...] = spectra_ref[...].astype(jnp.float32)
    for b in range(blocks):
        other[b * 256 : (b + 1) * 256, :] = spectra_ref[:, b * 256 : (b + 1) * 256].T
    acc[...] = jnp.zeros(acc.shape, jnp.float32)
    diagonal = lax.broadcasted_iota(jnp.int32, (32, 128), 0) == jnp.bitwise_and(
        lax.broadcasted_iota(jnp.int32, (32, 128), 1), 31
    )
    diagonal = jnp.where(diagonal, 1.0, 0.0)
    stack = stack_ids(inputs)

    def spread(rows):
        parts = []
        for u in range(GROUP):
            real = diagonal * rows[u : u + 1, :128]
            imag = diagonal * rows[u : u + 1, 128:]
            parts.append(jnp.concatenate([real, imag], axis=1))
            parts.append(jnp.concatenate([imag, -real], axis=1))
        return jnp.concatenate(parts, axis=0).astype(jnp.bfloat16)

    def step(g, carry):
        start = pl.multiple_of(g * GROUP, GROUP)
        products = []
        for b in range(blocks):
            right = other[b * 256 : (b + 1) * 256, :]
            products.append(
                [
                    jnp.dot(
                        spread(wide[pl.ds(start + p * half, GROUP), b * 256 : (b + 1) * 256]),
                        right,
                        preferred_element_type=jnp.float32,
                    )
                    for p in range(2)
                ]
            )
        row = lax.broadcasted_iota(jnp.int32, (GROUP, inputs), 0) + start
        col = lax.broadcasted_iota(jnp.int32, (GROUP, inputs), 1)
        apart = jnp.bitwise_and(col - row, inputs - 1)
        first = jnp.where((apart >= 1) & (apart <= half), 1.0, 0.0)
        signs = sign_ref[pl.ds(start, GROUP), :]
        goal = target_ref[pl.ds(start, GROUP), :].astype(jnp.bfloat16)
        values, members = [], []
        for u in range(GROUP):
            use = jnp.broadcast_to(first[u : u + 1], (32, inputs)) > 0.5
            sign = signs[u : u + 1]
            reals, imags = [], []
            for b in range(blocks):
                low, high = products[b]
                reals.append(
                    jnp.where(use, low[u * 64 : u * 64 + 32], high[u * 64 : u * 64 + 32])
                )
                imags.append(
                    sign
                    * jnp.where(use, low[u * 64 + 32 : u * 64 + 64], high[u * 64 + 32 : u * 64 + 64])
                )
            values.append(jnp.concatenate(reals + imags, axis=0).astype(jnp.bfloat16))
            members.append(one_hot(stack, goal[u : u + 1]))
        acc[...] += lax.dot_general(
            jnp.concatenate(members, axis=1),
            jnp.concatenate(values, axis=1),
            (((1,), (1,)), ((), ())),
            preferred_element_type=jnp.float32,
        )
        return carry

    lax.fori_loop(0, half // GROUP, step, 0)
    width = acc.shape[1]
    means = (acc[...] / jnp.maximum(count_ref[:, :width], 1.0)).astype(jnp.bfloat16)
    slots = out_ref.shape[0]
    slot_id = lax.broadcasted_iota(jnp.int32, (slots, STACK_ROWS), 0).astype(jnp.float32)
    place = jnp.where(slot_id == slot_ref[...], 1.0, 0.0).astype(jnp.bfloat16)
    out_ref[...] = jnp.dot(place, means, preferred_element_type=jnp.float32).astype(jnp.bfloat16)


def stack_means(spectra, target, sign, counts, slot, slots):
    inputs, lanes = spectra.shape
    width = lanes // SPECTRA
    return pl.pallas_call(
        stack_kernel,
        out_shape=jax.ShapeDtypeStruct((slots, width), jnp.bfloat16),
        scratch_shapes=[
            pltpu.VMEM((inputs, lanes), jnp.float32),
            pltpu.VMEM((lanes, inputs), jnp.bfloat16),
            pltpu.VMEM((STACK_ROWS, width), jnp.float32),
        ],
        compiler_params=pltpu.CompilerParams(vmem_limit_bytes=48 * MB),
        name="stack_means",
    )(spectra, target, sign, counts, slot)


def per_device(raw_samples, stack_code, stack_owner):
    feeds, chans = lax.axis_size("feed"), lax.axis_size("chan")
    inputs = raw_samples.shape[0]
    everyone = ("feed", "chan")
    share = CHANS // (feeds * chans)
    capacity = 2 * STACKS // feeds
    padded = -(-capacity // 16) * 16
    direct = share == FA and inputs == 8

    codes = lax.all_gather(stack_code, "feed", axis=0, tiled=True)
    owner = jnp.pad(
        stack_owner.astype(jnp.float32), (0, STACK_ROWS - STACKS), constant_values=-1.0
    )
    target, sign, counts, slot = targets(codes, owner.reshape(1, STACK_ROWS), padded)

    if direct:
        order = [c * feeds + f for f in range(feeds) for c in range(chans)]
        local = channelize(raw_samples, order).reshape(feeds * chans, inputs, 512)
    else:
        samples = jnp.pad(raw_samples, ((0, -inputs % 8), (0, 0)))
        local = channelize(samples, list(range(QS)))
        local = local.reshape(QS, samples.shape[0], 2, 2, SPECTRA, 32)[:, :inputs]
        local = local.transpose(0, 2, 5, 1, 3, 4).reshape(chans, feeds, share, inputs, 2, SPECTRA)
        local = local.transpose(1, 0, 3, 4, 5, 2).reshape(feeds * chans, inputs, 8 * share)
    moved = lax.all_to_all(local, everyone, split_axis=0, concat_axis=0, tiled=True)
    if not direct:
        moved = moved.reshape(feeds * chans, inputs, 8, share)
        moved = jnp.pad(moved, ((0, 0), (0, 0), (0, 0), (0, 32 - share)))
    moved = moved.reshape(feeds * chans * inputs, -1)

    means = stack_means(moved, target, sign, counts, slot, feeds * padded)
    means = means.reshape(feeds, padded, -1)
    landed = lax.all_to_all(means, "feed", split_axis=0, concat_axis=0, tiled=True)
    landed = landed[:, :capacity].reshape(feeds, capacity, 2, -1)[..., :share]
    return landed.transpose(1, 2, 0, 3).reshape(capacity, 2, feeds * share).astype(jnp.float32)


def solution(mesh):
    placed = (P(("feed", "chan"), None), P("feed", None), P())
    return jax.shard_map(
        per_device, mesh=mesh, in_specs=placed, out_specs=P("feed", None, "chan"), check_vma=False
    )
```

time: 323 us -> 69.7 us (0.22)
  other arithmetic: 105 us -> 0.05 us
  local copies, waits for them, and re-layouts: 104 us -> 6.55 us
  matrix products: 49.7 us -> 0 us
  Pallas kernels: 0 us -> 27 us
  waiting for transfers between devices: 22.7 us -> 0.01 us
  between operations: 15.1 us -> 0.09 us
  starting transfers between devices: 0.04 us -> 7.3 us
    scatter-add x1 -> x0, other arithmetic: 57 us -> none  [per_device(): jax.ops.segment_sum(jnp.ones((target.size,), jnp.float32), target.reshape...]
    dot_general x4 -> x0, matrix products: 49.7 us -> none  [the longest x1 31.4 us: stack_dense(): lax.dot_general(member, flattened, (((0,), (0,)), ((), ())), precision=la...]
    unnamed x11 -> x17, local copies, waits for them, and re-layouts: 48.6 us -> 5.54 us
    pallas_call x0 -> x3, Pallas kernels: none -> 27 us  [the longest x1 14.7 us: stack_means(): pl.pallas_call(stack_kernel, out_shape=jax.ShapeDtypeStruct((slots, width...]
    all_gather x1 -> x0, waiting for transfers between devices: 22.6 us -> none  [per_device(): pieces = lax.all_gather(own_block, 'feed', axis=0, tiled=True)]
    slice x1 -> x0, other arithmetic: 22.1 us -> none  [oriented(): values[:, :, 0]]
    another operation x5 -> x0, local copies, waits for them, and re-layouts: 19.1 us -> none  [the longest x1 11.1 us: oriented(): jnp.stack([values[:, :, 0], values[:, :, 1] * orient[:, :, None]], axis=2)]
    all_gather x0 -> x1, blocking collectives: none -> 17.4 us  [per_device(): codes = lax.all_gather(stack_code, 'feed', axis=0, tiled=True)]
  transfers between devices with their start and end apart: 2 -> 1, of which waited for: 1 -> 0; matrix products, arithmetic and copies ran while one was open for 21% -> 0% of each run, Pallas kernels for 0% -> 14%
where the time goes in v1:
time: 69.7 us; the launch traced here: 69.2 us
  blocking collectives  28.1 us (40%)
  Pallas kernels  27 us (39%)
  starting transfers between devices  7.3 us (10%)
  local copies, waits for them, and re-layouts  6.55 us (9%)
    all_gather x1, blocking collectives, per_device(): codes = lax.all_gather(stack_code, 'feed', axis=0, tiled=True)  17.4 us
    pallas_call x1, Pallas kernels, stack_means(): pl.pallas_call(stack_kernel, out_shape=jax.ShapeDtypeStruct((slots, width...  14.7 us
    all_to_all x1, blocking collectives, per_device(): lax.all_to_all(means, 'feed', split_axis=0, concat_axis=0, tiled=True)  10.7 us
    pallas_call x1, Pallas kernels, targets(): pl.pallas_call(functools.partial(targets_kernel, padded), out_shape=(jax....  9.49 us
    all_to_all x1, starting transfers between devices, per_device(): lax.all_to_all(local, everyone, split_axis=0, concat_axis=0, tiled=True)  7.3 us
    unnamed x17, local copies, waits for them, and re-layouts  5.54 us
    pallas_call x1, Pallas kernels, channelize(): pl.pallas_call(channelize_kernel, out_shape=jax.ShapeDtypeStruct((QS * in...  2.8 us
  transfers between devices with their start and end apart: 1, of which 0 were waited for; matrix products, arithmetic and copies ran while one was open for 0% of the time, Pallas kernels for 14%

profile of v1, /device:TPU:0, one launch (start us, length us, event | category | flops | bytes accessed | tf_op | source)
XLA Modules:
  0.0 69.2 jit_solution(12780285974922316597)
XLA Ops:
  0.0 0.0 copy-start
  0.0 1.4 %copy-done = bf16[8,90112]{1,0:T(8,128)(2,1)S(1)} copy-done((bf16[8,90112]{1,0:T(8,128)(2,1)S(1)}, bf16[8,90112]{1,0:T(8,128)(2,1)}, u32[]{:S(2)}) %copy-start) | copy-done | bytes 1441816
  1.4 0.0 copy-start.1
  1.4 0.9 %copy-done.1 = f32[8,8192]{1,0:T(8,128)S(1)} copy-done((f32[8,8192]{1,0:T(8,128)S(1)}, f32[8,8192]{1,0:T(8,128)}, u32[]{:S(2)}) %copy-start.1) | copy-done | bytes 262168
  2.3 0.0 copy-start.2
  2.3 0.8 %copy-done.2 = bf16[64,256]{1,0:T(8,128)(2,1)S(1)} copy-done((bf16[64,256]{1,0:T(8,128)(2,1)S(1)}, bf16[64,256]{1,0:T(8,128)(2,1)}, u32[]{:S(2)}) %copy-start.2) | copy-done | bytes 32792
  3.1 0.0 copy-start.3
  3.1 0.8 %copy-done.3 = f32[64,128]{1,0:T(8,128)S(1)} copy-done((f32[64,128]{1,0:T(8,128)S(1)}, f32[64,128]{1,0:T(8,128)}, u32[]{:S(2)}) %copy-start.3) | copy-done | bytes 32792
  3.8 0.0 copy-start.4
  3.8 0.8 %copy-done.4 = f32[64,128]{1,0:T(8,128)S(1)} copy-done((f32[64,128]{1,0:T(8,128)S(1)}, f32[64,128]{1,0:T(8,128)}, u32[]{:S(2)}) %copy-start.4) | copy-done | bytes 32792
  4.6 0.0 copy-start.5
  4.6 0.8 %copy-done.5 = bf16[128,64]{1,0:T(8,128)(2,1)S(1)} copy-done((bf16[128,64]{1,0:T(8,128)(2,1)S(1)}, bf16[128,64]{1,0:T(8,128)(2,1)}, u32[]{:S(2)}) %copy-start.5) | copy-done | bytes 16408
  5.3 0.0 copy-start.7
  5.3 0.0 copy-start.6
  5.4 2.8 %channelize.1 = bf16[256,512]{1,0:T(8,128)(2,1)} custom-call(bf16[8,90112]{1,0:T(8,128)(2,1)S(1)} %copy-done, f32[8,8192]{1,0:T(8,128)S(1)} %copy-done.1, bf16[128,64]{1,0:T(8,128)(2,1)S(1)} %copy-done.5, f32[64,128]{1,0:T(8,128)S(1)} %copy-done.4, f32[64,128]{1,0:T(8,128)S(1)} %copy-done.3, bf16[64,256]{1,0:T(8,128)(2,1)S(1)} %copy-done.2), custom_call_target="tpu_custom_call" | custom-call | tf_op jit(solution)/shard_map/channelize/pallas_call | solution.py:108
  8.2 7.3 %all-to-all-start = ((bf16[32,8,512]{2,1,0:T(8,128)(2,1)}), bf16[32,8,512]{2,1,0:T(8,128)(2,1)S(1)}, u32[]{:S(2)}, u32[]{:S(2)}) async-start(bf16[32,8,512]{2,1,0:T(8,128)(2,1)} %bitcast), calls=%async_computation | async-start | bytes 524288 | tf_op jit(solution)/shard_map/all_to_all | solution.py:303
  15.5 0.0 copy-done.7
  15.5 0.0 copy-done.6
  15.5 17.4 %all_gather.3.code_ref = s32[256,256]{1,0:T(8,128)S(1)} all-gather(s32[32,256]{1,0:T(8,128)S(1)} %copy-done.6), channel_id=1, replica_groups=mesh['feed'=8,'chan'=4] {'feed'}, dimensions={0}, use_global_device_ids=true | all-gather | bytes 294912 | tf_op jit(solution)/shard_map/all_gather | solution.py:288
  32.9 9.5 %targets.1 = (f32[128,256]{1,0:T(8,128)S(1)}, f32[128,256]{1,0:T(8,128)S(1)}, f32[384,128]{1,0:T(8,128)S(1)}, f32[1,384]{1,0:T(1,128)S(1)}) custom-call(s32[256,256]{1,0:T(8,128)S(1)} %all_gather.3.code_ref, f32[1,384]{1,0:T(1,128)S(1)} %reshape.20.owner_ref), custom_call_target="tpu_custom_call" | custom-call | tf_op jit(solution)/shard_map/targets/pallas_call | solution.py:172
  42.4 0.0 all-to-all-done
  42.4 14.7 %stack_means.1 = bf16[768,128]{1,0:T(8,128)(2,1)S(1)} custom-call(bf16[256,512]{1,0:T(8,128)(2,1)S(1)} %bitcast.9, f32[128,256]{1,0:T(8,128)S(1)} %get-tuple-element.9.target_ref, f32[128,256]{1,0:T(8,128)S(1)} %get-tuple-element.10.sign_ref, f32[384,128]{1,0:T(8,128)S(1)} %get-tuple-element.11.count_ref, f32[1,384]{1,0:T(1,128)S(1)} %get-tuple-element.12.slot_ref), custom_call_target="tpu_custom_call" | custom-call | tf_op jit(solution)/shard_map/stack_means/pallas_call | solution.py:266
  57.2 10.7 %all_to_all.10 = bf16[8,96,128]{2,1,0:T(8,128)(2,1)S(1)} all-to-all(bf16[8,96,128]{2,1,0:T(8,128)(2,1)S(1)} %bitcast.10), channel_id=1, replica_groups=mesh['feed'=8,'chan'=4] {'feed'}, dimensions={0} | all-to-all | bytes 393216 | tf_op jit(solution)/shard_map/all_to_all | solution.py:311
  67.9 0.2 copy.16
  68.2 1.0 %copy.15 = f32[95,2,512]{2,1,0:T(2,128)} copy(f32[95,2,512]{0,2,1:T(8,128)S(1)} %bitcast.11) | data formatting | bytes 778240 | tf_op jit(solution)/shard_map/convert_element_type | solution.py:313
  (5 shorter events, 0.1 us)
Async XLA Ops:
  0.0 1.4 %copy-start = (bf16[8,90112]{1,0:T(8,128)(2,1)S(1)}, bf16[8,90112]{1,0:T(8,128)(2,1)}, u32[]{:S(2)}) copy-start(bf16[8,90112]{1,0:T(8,128)(2,1)} %x_ref.1) | copy-start | bytes 4325380
  1.4 0.9 %copy-start.1 = (f32[8,8192]{1,0:T(8,128)S(1)}, f32[8,8192]{1,0:T(8,128)}, u32[]{:S(2)}) copy-start(f32[8,8192]{1,0:T(8,128)} %constant.12.clone.window_ref) | copy-start | bytes 786436
  2.3 0.8 %copy-start.2 = (bf16[64,256]{1,0:T(8,128)(2,1)S(1)}, bf16[64,256]{1,0:T(8,128)(2,1)}, u32[]{:S(2)}) copy-start(bf16[64,256]{1,0:T(8,128)(2,1)} %constant.16.clone.second_ref) | copy-start | bytes 98308
  3.1 0.8 %copy-start.3 = (f32[64,128]{1,0:T(8,128)S(1)}, f32[64,128]{1,0:T(8,128)}, u32[]{:S(2)}) copy-start(f32[64,128]{1,0:T(8,128)} %constant.15.clone.sin_ref) | copy-start | bytes 98308
  3.8 0.8 %copy-start.4 = (f32[64,128]{1,0:T(8,128)S(1)}, f32[64,128]{1,0:T(8,128)}, u32[]{:S(2)}) copy-start(f32[64,128]{1,0:T(8,128)} %constant.14.clone.cos_ref) | copy-start | bytes 98308
  4.6 0.8 %copy-start.5 = (bf16[128,64]{1,0:T(8,128)(2,1)S(1)}, bf16[128,64]{1,0:T(8,128)(2,1)}, u32[]{:S(2)}) copy-start(bf16[128,64]{1,0:T(8,128)(2,1)} %constant.13.clone.first_ref) | copy-start | bytes 49156
  5.3 10.1 %copy-start.7 = (s32[382]{0:T(512)S(1)}, s32[382]{0:T(512)}, u32[]{:S(2)}) copy-start(s32[382]{0:T(512)} %param.10) | copy-start | bytes 4588
  5.3 10.2 %copy-start.6 = (s32[32,256]{1,0:T(8,128)S(1)}, s32[32,256]{1,0:T(8,128)}, u32[]{:S(2)}) copy-start(s32[32,256]{1,0:T(8,128)} %param.9) | copy-start | bytes 98308
  8.2 34.3 %all-to-all-start = ((bf16[32,8,512]{2,1,0:T(8,128)(2,1)}), bf16[32,8,512]{2,1,0:T(8,128)(2,1)S(1)}, u32[]{:S(2)}, u32[]{:S(2)}) async-start(bf16[32,8,512]{2,1,0:T(8,128)(2,1)} %bitcast), calls=%async_computation | async-start | bytes 524288 | tf_op jit(solution)/shard_map/all_to_all | solution.py:303

commit v2 on v1

v2 whole, which is shorter than its diff:
```python
import functools
import math

import jax
import jax.numpy as jnp
import numpy as np
from jax import lax
from jax.experimental import pallas as pl
from jax.experimental.pallas import tpu as pltpu
from jax.sharding import PartitionSpec as P

SPECTRA = 4
TAPS = 8
FA = 64
FB = 128
FRAME = 8192
CHANS = 2048
STACKS = 382
QS = CHANS // FA
STACK_ROWS = 384
HALF_STACKS = 192
GROUP = 16
PIECES = 2
CODE_BASE = 384
MB = 1024 * 1024


def window_table():
    length = TAPS * FRAME
    sample = np.arange(length, dtype=np.float64)
    centred = (sample - length / 2 + 0.5) / FRAME
    hanning = 0.5 - 0.5 * np.cos(2.0 * np.pi * (sample + 0.5) / length)
    weights = np.sinc(centred) * hanning
    weights = weights * np.sqrt(FRAME / np.sum(weights * weights))
    return weights.reshape(TAPS, FRAME).astype(np.float32)


def angle_of(left_count, right_count, modulus):
    product = np.arange(left_count)[:, None] * np.arange(right_count)[None, :] % modulus
    return 2.0 * np.pi * product / modulus


def first_table():
    angles = angle_of(FA, FA, FA)
    return np.concatenate([np.cos(angles), -np.sin(angles)], axis=0)


def twiddles():
    angles = angle_of(FA, FB, FRAME)
    return np.cos(angles).astype(np.float32), np.sin(angles).astype(np.float32)


def second_table(order):
    angles = angle_of(FB, QS, FB).T[np.asarray(order)]
    cosine, sine = np.cos(angles), np.sin(angles)
    real_rows = np.concatenate([cosine, sine], axis=1)
    imag_rows = np.concatenate([-sine, cosine], axis=1)
    return np.concatenate([real_rows, imag_rows], axis=0)


def channelize_kernel(
    direct, x_hbm, code_hbm, window_hbm, first_hbm, cos_hbm, sin_hbm, second_hbm, out_ref,
    x_ref, code_ref, window_ref, first_ref, cos_ref, sin_ref, second_ref, frames, mixed, turned,
    x_sems, sems,
):
    inputs = x_ref.shape[0]
    piece = FRAME // PIECES
    pieces = []
    for k in range(PIECES):
        window_copy = pltpu.make_async_copy(
            window_hbm.at[:, k * piece : (k + 1) * piece],
            window_ref.at[:, k * piece : (k + 1) * piece],
            x_sems.at[k, 0],
        )
        window_copy.start()
        copies = [window_copy]
        for r in range(SPECTRA + TAPS - 1):
            at = slice(r * FRAME + k * piece, r * FRAME + (k + 1) * piece)
            copy = pltpu.make_async_copy(x_hbm.at[:, at], x_ref.at[:, at], x_sems.at[k, 1 + r])
            copy.start()
            copies.append(copy)
        pieces.append(copies)
    others = []
    for n, (source, target) in enumerate(
        [
            (code_hbm, code_ref),
            (first_hbm, first_ref),
            (cos_hbm, cos_ref),
            (sin_hbm, sin_ref),
            (second_hbm, second_ref),
        ]
    ):
        copy = pltpu.make_async_copy(source, target, sems.at[n])
        copy.start()
        others.append(copy)

    for a in range(FA):
        if a % (FA // PIECES) == 0:
            for copy in pieces[a // (FA // PIECES)]:
                copy.wait()
        sums = [None] * SPECTRA
        for r in range(SPECTRA + TAPS - 1):
            x = x_ref[:, r * FRAME + a * FB : r * FRAME + (a + 1) * FB].astype(jnp.float32)
            for t in range(SPECTRA):
                if 0 <= r - t < TAPS:
                    term = window_ref[r - t : r - t + 1, a * FB : (a + 1) * FB] * x
                    sums[t] = term if sums[t] is None else sums[t] + term
        for t in range(SPECTRA):
            frames[pl.ds(t * inputs * FA + a, inputs, stride=FA), :] = sums[t]
    for copy in others:
        copy.wait()

    count = code_ref.shape[1]
    half = count // 2
    place = lax.axis_index("feed") * lax.axis_size("chan") + lax.axis_index("chan")
    if direct:
        start = pl.multiple_of(lax.axis_index("chan") * inputs, 8)
        codes = code_ref[pl.ds(start, inputs), :]
        first_input = place * inputs
    else:
        codes = code_ref[...]
        first_input = place * (count // (lax.axis_size("feed") * lax.axis_size("chan")))
    row = lax.broadcasted_iota(jnp.int32, (inputs, half), 0) + first_input
    col = lax.broadcasted_iota(jnp.int32, (inputs, half), 1)
    apart = jnp.bitwise_and(col - row, count - 1)
    code = jnp.where((apart >= 1) & (apart <= half), codes[:, :half], codes[:, half:])
    shifted = code + CODE_BASE
    code = jnp.left_shift(128 + jnp.bitwise_and(shifted, 127), jnp.right_shift(shifted, 7))
    code = code.astype(jnp.float32)
    out_ref[:, 512:] = jnp.concatenate([code] * QS, axis=0).astype(jnp.bfloat16)

    for t in range(SPECTRA):
        rows = frames[t * inputs * FA : (t + 1) * inputs * FA, :].astype(jnp.bfloat16)
        wide = jnp.concatenate([rows[i * FA : (i + 1) * FA] for i in range(inputs)], axis=1)
        section = jnp.dot(first_ref[...], wide, preferred_element_type=jnp.float32)
        for i in range(inputs):
            real = section[:FA, i * FB : (i + 1) * FB]
            imag = section[FA:, i * FB : (i + 1) * FB]
            cosine, sine = cos_ref[...], sin_ref[...]
            twisted = jnp.concatenate(
                [real * cosine + imag * sine, imag * cosine - real * sine], axis=1
            ).astype(jnp.bfloat16)
            for h in range(2):
                start = ((i * 2 + h) * SPECTRA + t) * 32
                mixed[start : start + 32, :] = twisted[h * 32 : (h + 1) * 32]
    for i in range(inputs):
        spectra = lax.dot_general(
            second_ref[...],
            mixed[i * 256 : (i + 1) * 256, :],
            (((1,), (1,)), ((), ())),
            preferred_element_type=jnp.float32,
        ) * (1.0 / math.sqrt(FRAME))
        for m in range(2):
            for g in range(QS // 8):
                for h in range(2):
                    tile = spectra[m * QS + g * 8 : m * QS + g * 8 + 8, h * 128 : (h + 1) * 128]
                    start = ((h * 2 + m) * QS + g * 8) * inputs + i
                    turned[pl.ds(start, 8, stride=inputs), :] = tile
    for part in range(4):
        rows = turned[part * QS * inputs : (part + 1) * QS * inputs, :]
        out_ref[:, part * 128 : (part + 1) * 128] = rows.astype(jnp.bfloat16)


def channelize(samples, codes, order, direct):
    inputs = samples.shape[0]
    cosine, sine = twiddles()
    operands = (
        samples,
        codes,
        jnp.asarray(window_table()),
        jnp.asarray(first_table(), jnp.bfloat16),
        jnp.asarray(cosine),
        jnp.asarray(sine),
        jnp.asarray(second_table(order), jnp.bfloat16),
    )
    return pl.pallas_call(
        functools.partial(channelize_kernel, direct),
        out_shape=jax.ShapeDtypeStruct((QS * inputs, 512 + codes.shape[1] // 2), jnp.bfloat16),
        in_specs=[pl.BlockSpec(memory_space=pl.ANY)] * len(operands),
        scratch_shapes=[pltpu.VMEM(value.shape, value.dtype) for value in operands]
        + [
            pltpu.VMEM((SPECTRA * inputs * FA, FB), jnp.float32),
            pltpu.VMEM((SPECTRA * inputs * FA, 2 * FB), jnp.bfloat16),
            pltpu.VMEM((4 * QS * inputs, 128), jnp.float32),
            pltpu.SemaphoreType.DMA((PIECES, SPECTRA + TAPS)),
            pltpu.SemaphoreType.DMA((5,)),
        ],
        compiler_params=pltpu.CompilerParams(vmem_limit_bytes=56 * MB),
        name="channelize",
    )(*operands)


def stack_kernel(
    padded, data_ref, owner_ref, out_ref, wide, other, goal_ref, mask_ref, held, acc, tally
):
    inputs = data_ref.shape[0]
    half = inputs // 2
    lanes = data_ref.shape[1] - half
    blocks = lanes // 256
    width = lanes // SPECTRA
    steps = half // GROUP

    value = data_ref[:, lanes:].astype(jnp.float32).astype(jnp.int32)
    power = jnp.zeros(value.shape, jnp.int32)
    for e in range(1, 6):
        power = power + jnp.where(value >= 128 << e, 1, 0)
    code = power * 128 + jnp.right_shift(value, power) - 128 - CODE_BASE
    row = lax.broadcasted_iota(jnp.int32, (half, half), 0)
    col = lax.broadcasted_iota(jnp.int32, (half, half), 1)
    ahead = col > row
    low, high = code[:half], code[half:]
    code = jnp.concatenate([jnp.where(ahead, low, high), jnp.where(ahead, high, low)], axis=1)
    target = jnp.where(code >= 0, code, -1 - code)
    row = lax.broadcasted_iota(jnp.int32, (half, inputs), 0)
    col = lax.broadcasted_iota(jnp.int32, (half, inputs), 1)
    upper = target >= HALF_STACKS
    used = col != row
    goal_ref[...] = jnp.where(upper, target - HALF_STACKS, target).astype(jnp.float32)
    left = jnp.where(used & ~upper, 1.0, 0.0)
    right = jnp.where(used & upper, 1.0, 0.0)
    sign = jnp.where(code >= 0, 1.0, -1.0)
    for n, mask in enumerate((left, right, left * sign, right * sign)):
        mask_ref[n] = mask

    wide[...] = data_ref[:, :lanes].astype(jnp.float32)
    for b in range(blocks):
        other[b * 256 : (b + 1) * 256, :] = data_ref[:, b * 256 : (b + 1) * 256].T
    acc[...] = jnp.zeros(acc.shape, jnp.float32)
    tally[...] = jnp.zeros(tally.shape, jnp.float32)
    diagonal = lax.broadcasted_iota(jnp.int32, (32, 128), 0) == jnp.bitwise_and(
        lax.broadcasted_iota(jnp.int32, (32, 128), 1), 31
    )
    diagonal = jnp.where(diagonal, 1.0, 0.0)
    stack = lax.broadcasted_iota(jnp.int32, (HALF_STACKS, inputs), 0)
    stack = stack.astype(jnp.float32).astype(jnp.bfloat16)

    def spread(rows):
        parts = []
        for u in range(rows.shape[0]):
            real = diagonal * rows[u : u + 1, :128]
            imag = diagonal * rows[u : u + 1, 128:]
            parts.append(jnp.concatenate([real, imag], axis=1))
            parts.append(jnp.concatenate([imag, -real], axis=1))
        return jnp.concatenate(parts, axis=0).astype(jnp.bfloat16)

    def multiply(g):
        start = g * GROUP
        if not isinstance(g, int):
            start = pl.multiple_of(start, GROUP)
        row = lax.broadcasted_iota(jnp.int32, (GROUP, inputs), 0) + start
        col = lax.broadcasted_iota(jnp.int32, (GROUP, inputs), 1)
        apart = jnp.bitwise_and(col - row, inputs - 1)
        first = jnp.where((apart >= 1) & (apart <= half), 1.0, 0.0)
        for b in range(blocks):
            low = wide[pl.ds(start, GROUP), b * 256 : (b + 1) * 256]
            high = wide[pl.ds(start + half, GROUP), b * 256 : (b + 1) * 256]
            rows = [x[u : u + 1] for u in range(GROUP) for x in (low, high)]
            product = jnp.dot(
                spread(jnp.concatenate(rows, axis=0)),
                other[b * 256 : (b + 1) * 256, :],
                preferred_element_type=jnp.float32,
            )
            for u in range(GROUP):
                use = jnp.broadcast_to(first[u : u + 1], (64, inputs)) > 0.5
                at = u * 128
                chosen = jnp.where(use, product[at : at + 64], product[at + 64 : at + 128])
                chosen = chosen.astype(jnp.bfloat16)
                columns = slice(u * inputs, (u + 1) * inputs)
                held[b * 32 : b * 32 + 32, columns] = chosen[:32]
                at = (blocks + b) * 32
                held[at : at + 32, columns] = chosen[32:]

    def accumulate(g):
        start = g * GROUP
        if not isinstance(g, int):
            start = pl.multiple_of(start, GROUP)
        goal = goal_ref[pl.ds(start, GROUP), :].astype(jnp.bfloat16)
        masks = [mask_ref[n, pl.ds(start, GROUP), :].astype(jnp.bfloat16) for n in range(4)]
        members, values = [], []
        lefts = rights = None
        for u in range(GROUP):
            columns = slice(u * inputs, (u + 1) * inputs)
            left, right, left_sign, right_sign = [mask[u : u + 1] for mask in masks]
            real = held[: width // 2, columns]
            imag = held[width // 2 :, columns]
            values.append(
                jnp.concatenate(
                    [real * left, imag * left_sign, real * right, imag * right_sign], axis=0
                )
            )
            member = jnp.where(
                stack == goal[u : u + 1], jnp.ones_like(stack), jnp.zeros_like(stack)
            )
            members.append(member)
            lefts = member * left if lefts is None else lefts + member * left
            rights = member * right if rights is None else rights + member * right
        acc[...] += lax.dot_general(
            jnp.concatenate(members, axis=1),
            jnp.concatenate(values, axis=1),
            (((1,), (1,)), ((), ())),
            preferred_element_type=jnp.float32,
        )
        tally[0] += lefts.astype(jnp.float32)
        tally[1] += rights.astype(jnp.float32)

    def step(g, carry):
        accumulate(g)
        multiply(g + 1)
        return carry

    multiply(0)
    lax.fori_loop(0, steps - 1, step, 0)
    accumulate(steps - 1)

    owner = owner_ref[...]
    across = jnp.broadcast_to(owner, (STACK_ROWS, STACK_ROWS))
    down = across.T
    before = lax.broadcasted_iota(jnp.int32, (STACK_ROWS, STACK_ROWS), 0)
    after = lax.broadcasted_iota(jnp.int32, (STACK_ROWS, STACK_ROWS), 1)
    earlier = jnp.where((across == down) & (before < after), 1.0, 0.0)
    rank = jnp.sum(earlier, axis=0, keepdims=True)
    slot = jnp.where(owner >= 0, owner * padded, -STACK_ROWS) + rank

    means = []
    for n in range(2):
        counts = jnp.maximum(jnp.sum(tally[n], axis=1, keepdims=True), 1.0)
        means.append((acc[:, n * width : (n + 1) * width] / counts).astype(jnp.bfloat16))
    means = jnp.concatenate(means, axis=0)
    slots = out_ref.shape[0]
    slot_id = lax.broadcasted_iota(jnp.int32, (slots, STACK_ROWS), 0).astype(jnp.float32)
    place = jnp.where(slot_id == slot, 1.0, 0.0).astype(jnp.bfloat16)
    out_ref[...] = jnp.dot(place, means, preferred_element_type=jnp.float32).astype(jnp.bfloat16)


def stack_means(data, owner, padded, feeds):
    inputs = data.shape[0]
    half = inputs // 2
    lanes = data.shape[1] - half
    width = lanes // SPECTRA
    return pl.pallas_call(
        functools.partial(stack_kernel, padded),
        out_shape=jax.ShapeDtypeStruct((feeds * padded, width), jnp.bfloat16),
        scratch_shapes=[
            pltpu.VMEM((inputs, lanes), jnp.float32),
            pltpu.VMEM((lanes, inputs), jnp.bfloat16),
            pltpu.VMEM((half, inputs), jnp.float32),
            pltpu.VMEM((4, half, inputs), jnp.float32),
            pltpu.VMEM((width, GROUP * inputs), jnp.bfloat16),
            pltpu.VMEM((HALF_STACKS, 2 * width), jnp.float32),
            pltpu.VMEM((2, HALF_STACKS, inputs), jnp.float32),
        ],
        compiler_params=pltpu.CompilerParams(vmem_limit_bytes=48 * MB),
        name="stack_means",
    )(data, owner)


def lay_out_kernel(feeds, padded, capacity, landed_ref, out_ref):
    lane = lax.broadcasted_iota(jnp.int32, (padded, 128), 1)
    for pair in range(feeds // 2):
        left = landed_ref[2 * pair * padded : (2 * pair + 1) * padded, :].astype(jnp.float32)
        right = landed_ref[(2 * pair + 1) * padded : (2 * pair + 2) * padded, :].astype(
            jnp.float32
        )
        real = jnp.where(lane < 64, left, pltpu.roll(right, 64, 1))
        imag = jnp.where(lane < 64, pltpu.roll(left, 64, 1), right)
        for part, value in enumerate((real, imag)):
            out_ref[pl.ds(pair * 2 + part, capacity, stride=feeds), :] = value[:capacity]


def lay_out(landed, feeds, padded, capacity):
    return pl.pallas_call(
        functools.partial(lay_out_kernel, feeds, padded, capacity),
        out_shape=jax.ShapeDtypeStruct((capacity * feeds, 128), jnp.float32),
        compiler_params=pltpu.CompilerParams(vmem_limit_bytes=32 * MB),
        name="lay_out",
    )(landed)


def per_device(raw_samples, stack_code, stack_owner):
    feeds, chans = lax.axis_size("feed"), lax.axis_size("chan")
    devices = feeds * chans
    inputs = raw_samples.shape[0]
    half = stack_code.shape[1] // 2
    everyone = ("feed", "chan")
    share = CHANS // devices
    capacity = 2 * STACKS // feeds
    padded = -(-capacity // 16) * 16
    direct = share == FA and inputs == 8

    owner = jnp.pad(
        stack_owner.astype(jnp.float32), (0, STACK_ROWS - STACKS), constant_values=-1.0
    ).reshape(1, STACK_ROWS)

    if direct:
        order = [c * feeds + f for f in range(feeds) for c in range(chans)]
        local = channelize(raw_samples, stack_code, order, True)
        local = local.reshape(devices, inputs, -1)
    else:
        samples = jnp.pad(raw_samples, ((0, -inputs % 8), (0, 0)))
        codes = lax.dynamic_slice_in_dim(stack_code, lax.axis_index("chan") * inputs, inputs)
        codes = jnp.pad(codes, ((0, -inputs % 8), (0, 0)))
        local = channelize(samples, codes, list(range(QS)), False)
        local = local.reshape(QS, samples.shape[0], -1)[:, :inputs]
        codes = jnp.broadcast_to(local[:1, :, 512:], (devices, inputs, half))
        local = local[:, :, :512].reshape(QS, inputs, 2, 2, SPECTRA, 32)
        local = local.transpose(0, 2, 5, 1, 3, 4).reshape(chans, feeds, share, inputs, 2, SPECTRA)
        local = local.transpose(1, 0, 3, 4, 5, 2).reshape(devices, inputs, 8 * share)
        local = jnp.concatenate([local, codes], axis=2)
    moved = lax.all_to_all(local, everyone, split_axis=0, concat_axis=0, tiled=True)
    if not direct:
        codes = moved[:, :, 8 * share :]
        moved = moved[:, :, : 8 * share].reshape(devices, inputs, 8, share)
        moved = jnp.pad(moved, ((0, 0), (0, 0), (0, 0), (0, 32 - share)))
        moved = jnp.concatenate([moved.reshape(devices, inputs, 256), codes], axis=2)
    moved = moved.reshape(devices * inputs, -1)

    means = stack_means(moved, owner, padded, feeds)
    means = means.reshape(feeds, padded, -1)
    landed = lax.all_to_all(means, "feed", split_axis=0, concat_axis=0, tiled=True)
    if direct:
        landed = lay_out(landed.reshape(feeds * padded, -1), feeds, padded, capacity)
        landed = landed.reshape(capacity, feeds // 2, 2, 128).transpose(0, 2, 1, 3)
        return landed.reshape(capacity, 2, feeds * share)
    landed = landed[:, :capacity].reshape(feeds, capacity, 2, -1)[..., :share]
    return landed.transpose(1, 2, 0, 3).reshape(capacity, 2, feeds * share).astype(jnp.float32)


def solution(mesh):
    placed = (P(("feed", "chan"), None), P("feed", None), P())
    return jax.shard_map(
        per_device, mesh=mesh, in_specs=placed, out_specs=P("feed", None, "chan"), check_vma=False
    )
```

time: 69.7 us -> 47.8 us (0.69)
  blocking collectives: 28.1 us -> 10.9 us
  waiting for transfers between devices: 0.01 us -> 12.2 us
  Pallas kernels: 27 us -> 17 us
  local copies, waits for them, and re-layouts: 6.55 us -> 0.01 us
    all_gather x1 -> x0, blocking collectives: 17.4 us -> none  [per_device(): codes = lax.all_gather(stack_code, 'feed', axis=0, tiled=True)]
    all_to_all x1, waiting for transfers between devices: 0.01 us -> 12.2 us  [per_device(): lax.all_to_all(local, everyone, split_axis=0, concat_axis=0, tiled=True)]
    pallas_call x3, Pallas kernels: 27 us -> 17 us  [the longest x1 11.9 us: stack_means(): pl.pallas_call(functools.partial(stack_kernel, padded), out_shape=jax.Sha...]
    unnamed x17 -> x2, local copies, waits for them, and re-layouts: 5.54 us -> 0.01 us
    convert_element_type x2 -> x0, local copies, waits for them, and re-layouts: 1 us -> none  [per_device(): landed.transpose(1, 2, 0, 3).reshape(capacity, 2, feeds * share)]
  transfers between devices with their start and end apart: 1 -> 1, of which waited for: 0 -> 1; matrix products, arithmetic and copies ran while one was open for 0% -> 0% of each run, Pallas kernels for 14% -> 0%
where the time goes in v2:
time: 47.8 us; the launch traced here: 47.6 us
  Pallas kernels  17 us (36%)
  waiting for transfers between devices  12.2 us (26%)
  blocking collectives  10.9 us (23%)
  starting transfers between devices  7.3 us (15%)
    all_to_all x1, waiting for transfers between devices, per_device(): lax.all_to_all(local, everyone, split_axis=0, concat_axis=0, tiled=True)  12.2 us
    pallas_call x1, Pallas kernels, stack_means(): pl.pallas_call(functools.partial(stack_kernel, padded), out_shape=jax.Sha...  11.9 us
    all_to_all x1, blocking collectives, per_device(): lax.all_to_all(means, 'feed', split_axis=0, concat_axis=0, tiled=True)  10.9 us
    all_to_all x1, starting transfers between devices, per_device(): lax.all_to_all(local, everyone, split_axis=0, concat_axis=0, tiled=True)  7.3 us
    pallas_call x1, Pallas kernels, channelize(): pl.pallas_call(functools.partial(channelize_kernel, direct), out_shape=ja...  4.15 us
  transfers between devices with their start and end apart: 1, of which 1 were waited for; matrix products, arithmetic and copies ran while one was open for 0% of the time, Pallas kernels for 0%

profile of v2, /device:TPU:0, one launch (start us, length us, event | category | flops | bytes accessed | tf_op | source)
XLA Modules:
  0.0 47.6 jit_solution(1693059260186066265)
XLA Ops:
  0.0 0.0 copy-start
  0.0 4.2 %channelize.1 = bf16[256,640]{1,0:T(8,128)(2,1)} custom-call(bf16[8,90112]{1,0:T(8,128)(2,1)} %x_hbm.1, s32[32,256]{1,0:T(8,128)} %code_hbm.1, f32[8,8192]{1,0:T(8,128)} %constant.12.clone.window_hbm, bf16[128,64]{1,0:T(8,128)(2,1)} %constant.13.clone.first_hbm, f32[64,128]{1,0:T(8,128)} %constant.14.clone.cos_hbm, f32[64,128]{1,0:T(8,128)} %constant.15.clone.sin_hbm, ...), custom_call_target="tpu_custom_call" | custom-call | tf_op jit(solution)/shard_map/channelize/pallas_call | solution.py:176
  4.2 7.3 %all-to-all-start = ((bf16[32,8,640]{2,1,0:T(8,128)(2,1)}), bf16[32,8,640]{2,1,0:T(8,128)(2,1)S(1)}, u32[]{:S(2)}, u32[]{:S(2)}) async-start(bf16[32,8,640]{2,1,0:T(8,128)(2,1)} %bitcast.12), calls=%async_computation | async-start | bytes 655360 | tf_op jit(solution)/shard_map/all_to_all | solution.py:409
  11.5 0.0 copy-done
  11.5 12.2 %all-to-all-done = bf16[32,8,640]{2,1,0:T(8,128)(2,1)S(1)} async-done(((bf16[32,8,640]{2,1,0:T(8,128)(2,1)}), bf16[32,8,640]{2,1,0:T(8,128)(2,1)S(1)}, u32[]{:S(2)}, u32[]{:S(2)}) %all-to-all-start) | async-done | bytes 327712 | tf_op jit(solution)/shard_map/all_to_all | solution.py:409
  23.8 11.9 %stack_means.1 = bf16[768,128]{1,0:T(8,128)(2,1)S(1)} custom-call(bf16[256,640]{1,0:T(8,128)(2,1)S(1)} %bitcast.9, f32[1,384]{1,0:T(1,128)S(1)} %reshape.23.owner_ref), custom_call_target="tpu_custom_call" | custom-call | tf_op jit(solution)/shard_map/stack_means/pallas_call | solution.py:340
  35.7 10.9 %all_to_all.10 = bf16[8,96,128]{2,1,0:T(8,128)(2,1)S(1)} all-to-all(bf16[8,96,128]{2,1,0:T(8,128)(2,1)S(1)} %bitcast.10), channel_id=1, replica_groups=mesh['feed'=8,'chan'=4] {'feed'}, dimensions={0} | all-to-all | bytes 393216 | tf_op jit(solution)/shard_map/all_to_all | solution.py:419
  46.7 0.9 %lay_out.1 = f32[760,128]{1,0:T(8,128)} custom-call(bf16[768,128]{1,0:T(8,128)(2,1)S(1)} %bitcast.11), custom_call_target="tpu_custom_call" | custom-call | tf_op jit(solution)/shard_map/lay_out/pallas_call | solution.py:371
  (3 shorter events, 0.0 us)
Async XLA Ops:
  0.0 11.5 %copy-start = (s32[382]{0:T(512)S(1)}, s32[382]{0:T(512)}, u32[]{:S(2)}) copy-start(s32[382]{0:T(512)} %param.10) | copy-start | bytes 4588
  4.2 19.6 %all-to-all-start = ((bf16[32,8,640]{2,1,0:T(8,128)(2,1)}), bf16[32,8,640]{2,1,0:T(8,128)(2,1)S(1)}, u32[]{:S(2)}, u32[]{:S(2)}) async-start(bf16[32,8,640]{2,1,0:T(8,128)(2,1)} %bitcast.12), calls=%async_computation | async-start | bytes 655360 | tf_op jit(solution)/shard_map/all_to_all | solution.py:409

commit v3 on v2

--- a/solution.py
+++ b/solution.py
@@ -21,6 +21,7 @@
 HALF_STACKS = 192
 GROUP = 16
 PIECES = 2
+PARTS = (slice(0, GROUP),)
 CODE_BASE = 384
 MB = 1024 * 1024
 
@@ -106,7 +107,7 @@
                     term = window_ref[r - t : r - t + 1, a * FB : (a + 1) * FB] * x
                     sums[t] = term if sums[t] is None else sums[t] + term
         for t in range(SPECTRA):
-            frames[pl.ds(t * inputs * FA + a, inputs, stride=FA), :] = sums[t]
+            frames[(t * FA + a) * inputs : (t * FA + a + 1) * inputs, :] = sums[t]
     for copy in others:
         copy.wait()
 
@@ -130,8 +131,8 @@
     out_ref[:, 512:] = jnp.concatenate([code] * QS, axis=0).astype(jnp.bfloat16)
 
     for t in range(SPECTRA):
-        rows = frames[t * inputs * FA : (t + 1) * inputs * FA, :].astype(jnp.bfloat16)
-        wide = jnp.concatenate([rows[i * FA : (i + 1) * FA] for i in range(inputs)], axis=1)
+        wide = [frames[pl.ds(t * FA * inputs + i, FA, stride=inputs), :] for i in range(inputs)]
+        wide = jnp.concatenate([part.astype(jnp.bfloat16) for part in wide], axis=1)
         section = jnp.dot(first_ref[...], wide, preferred_element_type=jnp.float32)
         for i in range(inputs):
             real = section[:FA, i * FB : (i + 1) * FB]
@@ -140,9 +141,9 @@
             twisted = jnp.concatenate(
                 [real * cosine + imag * sine, imag * cosine - real * sine], axis=1
             ).astype(jnp.bfloat16)
-            for h in range(2):
-                start = ((i * 2 + h) * SPECTRA + t) * 32
-                mixed[start : start + 32, :] = twisted[h * 32 : (h + 1) * 32]
+            for part in range(4):
+                start = (i * 4 + part) * 64 + t * 16
+                mixed[start : start + 16, :] = twisted[part * 16 : (part + 1) * 16]
     for i in range(inputs):
         spectra = lax.dot_general(
             second_ref[...],
@@ -190,8 +191,30 @@
     )(*operands)
 
 
+def place_kernel(padded, owner_ref, place_ref):
+    owner = owner_ref[...]
+    across = jnp.broadcast_to(owner, (STACK_ROWS, STACK_ROWS))
+    down = across.T
+    before = lax.broadcasted_iota(jnp.int32, (STACK_ROWS, STACK_ROWS), 0)
+    after = lax.broadcasted_iota(jnp.int32, (STACK_ROWS, STACK_ROWS), 1)
+    earlier = jnp.where((across == down) & (before < after), 1.0, 0.0)
+    rank = jnp.sum(earlier, axis=0, keepdims=True)
+    slot = jnp.where(owner >= 0, owner * padded, -STACK_ROWS) + rank
+    slot_id = lax.broadcasted_iota(jnp.int32, place_ref.shape, 0).astype(jnp.float32)
+    place_ref[...] = jnp.where(slot_id == slot, 1.0, 0.0).astype(jnp.bfloat16)
+
+
+def place_stacks(owner, padded, feeds):
+    return pl.pallas_call(
+        functools.partial(place_kernel, padded),
+        out_shape=jax.ShapeDtypeStruct((feeds * padded, STACK_ROWS), jnp.bfloat16),
+        compiler_params=pltpu.CompilerParams(vmem_limit_bytes=16 * MB),
+        name="place_stacks",
+    )(owner)
+
+
 def stack_kernel(
-    padded, data_ref, owner_ref, out_ref, wide, other, goal_ref, mask_ref, held, acc, tally
+    data_ref, place_ref, out_ref, wide, pairs, other, twin, goal_ref, mask_ref, held, acc, tally
 ):
     inputs = data_ref.shape[0]
     half = inputs // 2
@@ -208,7 +231,8 @@
     row = lax.broadcasted_iota(jnp.int32, (half, half), 0)
     col = lax.broadcasted_iota(jnp.int32, (half, half), 1)
     ahead = col > row
-    low, high = code[:half], code[half:]
+    low = code[:half]
+    high = -1 - code[half:].astype(jnp.float32).T.astype(jnp.int32)
     code = jnp.concatenate([jnp.where(ahead, low, high), jnp.where(ahead, high, low)], axis=1)
     target = jnp.where(code >= 0, code, -1 - code)
     row = lax.broadcasted_iota(jnp.int32, (half, inputs), 0)
@@ -222,58 +246,98 @@
     for n, mask in enumerate((left, right, left * sign, right * sign)):
         mask_ref[n] = mask
 
-    wide[...] = data_ref[:, :lanes].astype(jnp.float32)
+    lane = lax.broadcasted_iota(jnp.int32, (half // 2, 128), 1)
+    twin[...] = jnp.zeros(twin.shape, jnp.bfloat16)
     for b in range(blocks):
         other[b * 256 : (b + 1) * 256, :] = data_ref[:, b * 256 : (b + 1) * 256].T
+        for m in range(2):
+            tile = b * 2 + m
+            wide[tile * inputs : (tile + 1) * inputs, :] = data_ref[
+                :, tile * 128 : (tile + 1) * 128
+            ].astype(jnp.float32)
+            even = wide[pl.ds(tile * inputs + half, half // 2, stride=2), :]
+            odd = wide[pl.ds(tile * inputs + half + 1, half // 2, stride=2), :]
+            for part in range(2):
+                if part == 0:
+                    both = jnp.where(lane < 64, even, pltpu.roll(odd, 64, 1))
+                else:
+                    both = jnp.where(lane < 64, pltpu.roll(even, 64, 1), odd)
+                at = (tile * 2 + part) * (half // 2)
+                pairs[at : at + half // 2, :] = both
+                source = slice(tile * 128 + part * 64, tile * 128 + part * 64 + 64)
+                for side in range(2):
+                    at = (b * 2 + part) * 256 + m * 128 + side * 64
+                    twin[at : at + 64, side * half : (side + 1) * half] = other[source, half:]
     acc[...] = jnp.zeros(acc.shape, jnp.float32)
     tally[...] = jnp.zeros(tally.shape, jnp.float32)
-    diagonal = lax.broadcasted_iota(jnp.int32, (32, 128), 0) == jnp.bitwise_and(
-        lax.broadcasted_iota(jnp.int32, (32, 128), 1), 31
-    )
-    diagonal = jnp.where(diagonal, 1.0, 0.0)
+
+    def diagonal(rows):
+        row = lax.broadcasted_iota(jnp.int32, (rows, 128), 0)
+        lane = lax.broadcasted_iota(jnp.int32, (rows, 128), 1)
+        channel = jnp.bitwise_and(lane, 15)
+        if rows == 32:
+            channel = channel + jnp.where(lane >= 64, 16, 0)
+        return jnp.where(row == channel, 1.0, 0.0)
+
+    diagonal_32, diagonal_16 = diagonal(32), diagonal(16)
     stack = lax.broadcasted_iota(jnp.int32, (HALF_STACKS, inputs), 0)
     stack = stack.astype(jnp.float32).astype(jnp.bfloat16)
 
-    def spread(rows):
+    def spread(reals, imags, mask):
         parts = []
-        for u in range(rows.shape[0]):
-            real = diagonal * rows[u : u + 1, :128]
-            imag = diagonal * rows[u : u + 1, 128:]
+        for u in range(reals.shape[0]):
+            real = mask * reals[u : u + 1]
+            imag = mask * imags[u : u + 1]
             parts.append(jnp.concatenate([real, imag], axis=1))
             parts.append(jnp.concatenate([imag, -real], axis=1))
         return jnp.concatenate(parts, axis=0).astype(jnp.bfloat16)
 
+    def at_step(g, rows):
+        return g * rows if isinstance(g, int) else pl.multiple_of(g * rows, rows)
+
     def multiply(g):
-        start = g * GROUP
-        if not isinstance(g, int):
-            start = pl.multiple_of(start, GROUP)
-        row = lax.broadcasted_iota(jnp.int32, (GROUP, inputs), 0) + start
-        col = lax.broadcasted_iota(jnp.int32, (GROUP, inputs), 1)
-        apart = jnp.bitwise_and(col - row, inputs - 1)
-        first = jnp.where((apart >= 1) & (apart <= half), 1.0, 0.0)
+        start = at_step(g, GROUP)
+        start_pair = at_step(g, GROUP // 2)
+        row = lax.broadcasted_iota(jnp.int32, (GROUP, half), 0) + start
+        col = lax.broadcasted_iota(jnp.int32, (GROUP, half), 1)
+        ahead = jnp.where(col > row, 1.0, 0.0)
         for b in range(blocks):
-            low = wide[pl.ds(start, GROUP), b * 256 : (b + 1) * 256]
-            high = wide[pl.ds(start + half, GROUP), b * 256 : (b + 1) * 256]
-            rows = [x[u : u + 1] for u in range(GROUP) for x in (low, high)]
+            rows = [wide[pl.ds((b * 2 + m) * inputs + start, GROUP), :] for m in range(2)]
             product = jnp.dot(
-                spread(jnp.concatenate(rows, axis=0)),
+                spread(rows[0], rows[1], diagonal_32),
                 other[b * 256 : (b + 1) * 256, :],
                 preferred_element_type=jnp.float32,
             )
+            lower = []
+            for part in range(2):
+                rows = [
+                    pairs[
+                        pl.ds(((b * 2 + m) * 2 + part) * (half // 2) + start_pair, GROUP // 2), :
+                    ]
+                    for m in range(2)
+                ]
+                at = (b * 2 + part) * 256
+                lower.append(
+                    jnp.dot(
+                        spread(rows[0], rows[1], diagonal_16),
+                        twin[at : at + 256, :],
+                        preferred_element_type=jnp.float32,
+                    )
+                )
             for u in range(GROUP):
-                use = jnp.broadcast_to(first[u : u + 1], (64, inputs)) > 0.5
-                at = u * 128
-                chosen = jnp.where(use, product[at : at + 64], product[at + 64 : at + 128])
-                chosen = chosen.astype(jnp.bfloat16)
-                columns = slice(u * inputs, (u + 1) * inputs)
-                held[b * 32 : b * 32 + 32, columns] = chosen[:32]
-                at = (blocks + b) * 32
-                held[at : at + 32, columns] = chosen[32:]
+                side = slice((u % 2) * half, (u % 2 + 1) * half)
+                use = jnp.broadcast_to(ahead[u : u + 1], (32, half)) > 0.5
+                for p in range(2):
+                    mine = product[u * 64 + p * 32 : u * 64 + p * 32 + 32]
+                    at = (u // 2) * 32 + p * 16
+                    low = jnp.concatenate([x[at : at + 16, side] for x in lower], axis=0)
+                    chosen = jnp.where(use, mine[:, :half], low)
+                    both = jnp.concatenate([chosen, mine[:, half:]], axis=1)
+                    at = (p * blocks + b) * 32
+                    held[at : at + 32, u * inputs : (u + 1) * inputs] = both.astype(jnp.bfloat16)
 
     def accumulate(g):
-        start = g * GROUP
-        if not isinstance(g, int):
-            start = pl.multiple_of(start, GROUP)
+        start = at_step(g, GROUP)
         goal = goal_ref[pl.ds(start, GROUP), :].astype(jnp.bfloat16)
         masks = [mask_ref[n, pl.ds(start, GROUP), :].astype(jnp.bfloat16) for n in range(4)]
         members, values = [], []
@@ -294,12 +358,13 @@
             members.append(member)
             lefts = member * left if lefts is None else lefts + member * left
             rights = member * right if rights is None else rights + member * right
-        acc[...] += lax.dot_general(
-            jnp.concatenate(members, axis=1),
-            jnp.concatenate(values, axis=1),
-            (((1,), (1,)), ((), ())),
-            preferred_element_type=jnp.float32,
-        )
+        for n, part in enumerate(PARTS):
+            acc[n] += lax.dot_general(
+                jnp.concatenate(members[part], axis=1),
+                jnp.concatenate(values[part], axis=1),
+                (((1,), (1,)), ((), ())),
+                preferred_element_type=jnp.float32,
+            )
         tally[0] += lefts.astype(jnp.float32)
         tally[1] += rights.astype(jnp.float32)
 
@@ -312,46 +377,38 @@
     lax.fori_loop(0, steps - 1, step, 0)
     accumulate(steps - 1)
 
-    owner = owner_ref[...]
-    across = jnp.broadcast_to(owner, (STACK_ROWS, STACK_ROWS))
-    down = across.T
-    before = lax.broadcasted_iota(jnp.int32, (STACK_ROWS, STACK_ROWS), 0)
-    after = lax.broadcasted_iota(jnp.int32, (STACK_ROWS, STACK_ROWS), 1)
-    earlier = jnp.where((across == down) & (before < after), 1.0, 0.0)
-    rank = jnp.sum(earlier, axis=0, keepdims=True)
-    slot = jnp.where(owner >= 0, owner * padded, -STACK_ROWS) + rank
-
     means = []
     for n in range(2):
         counts = jnp.maximum(jnp.sum(tally[n], axis=1, keepdims=True), 1.0)
-        means.append((acc[:, n * width : (n + 1) * width] / counts).astype(jnp.bfloat16))
+        total = sum(acc[k, :, n * width : (n + 1) * width] for k in range(len(PARTS)))
+        means.append((total / counts).astype(jnp.bfloat16))
     means = jnp.concatenate(means, axis=0)
-    slots = out_ref.shape[0]
-    slot_id = lax.broadcasted_iota(jnp.int32, (slots, STACK_ROWS), 0).astype(jnp.float32)
-    place = jnp.where(slot_id == slot, 1.0, 0.0).astype(jnp.bfloat16)
-    out_ref[...] = jnp.dot(place, means, preferred_element_type=jnp.float32).astype(jnp.bfloat16)
-
-
-def stack_means(data, owner, padded, feeds):
+    moved = jnp.dot(place_ref[...], means, preferred_element_type=jnp.float32)
+    out_ref[...] = moved.astype(jnp.bfloat16)
+
+
+def stack_means(data, place):
     inputs = data.shape[0]
     half = inputs // 2
     lanes = data.shape[1] - half
     width = lanes // SPECTRA
     return pl.pallas_call(
-        functools.partial(stack_kernel, padded),
-        out_shape=jax.ShapeDtypeStruct((feeds * padded, width), jnp.bfloat16),
+        stack_kernel,
+        out_shape=jax.ShapeDtypeStruct((place.shape[0], width), jnp.bfloat16),
         scratch_shapes=[
-            pltpu.VMEM((inputs, lanes), jnp.float32),
+            pltpu.VMEM((lanes // 128 * inputs, 128), jnp.float32),
+            pltpu.VMEM((lanes // 128 * half, 128), jnp.float32),
             pltpu.VMEM((lanes, inputs), jnp.bfloat16),
+            pltpu.VMEM((2 * lanes, inputs), jnp.bfloat16),
             pltpu.VMEM((half, inputs), jnp.float32),
             pltpu.VMEM((4, half, inputs), jnp.float32),
             pltpu.VMEM((width, GROUP * inputs), jnp.bfloat16),
-            pltpu.VMEM((HALF_STACKS, 2 * width), jnp.float32),
+            pltpu.VMEM((len(PARTS), HALF_STACKS, 2 * width), jnp.float32),
             pltpu.VMEM((2, HALF_STACKS, inputs), jnp.float32),
         ],
         compiler_params=pltpu.CompilerParams(vmem_limit_bytes=48 * MB),
         name="stack_means",
-    )(data, owner)
+    )(data, place)
 
 
 def lay_out_kernel(feeds, padded, capacity, landed_ref, out_ref):
@@ -390,6 +447,7 @@
     owner = jnp.pad(
         stack_owner.astype(jnp.float32), (0, STACK_ROWS - STACKS), constant_values=-1.0
     ).reshape(1, STACK_ROWS)
+    place = place_stacks(owner, padded, feeds)
 
     if direct:
         order = [c * feeds + f for f in range(feeds) for c in range(chans)]
@@ -402,19 +460,20 @@
         local = channelize(samples, codes, list(range(QS)), False)
         local = local.reshape(QS, samples.shape[0], -1)[:, :inputs]
         codes = jnp.broadcast_to(local[:1, :, 512:], (devices, inputs, half))
-        local = local[:, :, :512].reshape(QS, inputs, 2, 2, SPECTRA, 32)
-        local = local.transpose(0, 2, 5, 1, 3, 4).reshape(chans, feeds, share, inputs, 2, SPECTRA)
-        local = local.transpose(1, 0, 3, 4, 5, 2).reshape(devices, inputs, 8 * share)
+        local = local[:, :, :512].reshape(QS, inputs, 2, 2, 2, SPECTRA, 16)
+        local = local.transpose(0, 2, 4, 6, 1, 3, 5)
+        local = local.reshape(chans, feeds, share // 16, 16, inputs, 2, SPECTRA)
+        local = local.transpose(1, 0, 4, 5, 2, 6, 3).reshape(devices, inputs, 8 * share)
         local = jnp.concatenate([local, codes], axis=2)
     moved = lax.all_to_all(local, everyone, split_axis=0, concat_axis=0, tiled=True)
     if not direct:
         codes = moved[:, :, 8 * share :]
-        moved = moved[:, :, : 8 * share].reshape(devices, inputs, 8, share)
-        moved = jnp.pad(moved, ((0, 0), (0, 0), (0, 0), (0, 32 - share)))
+        moved = moved[:, :, : 8 * share].reshape(devices, inputs, 2, 4 * share)
+        moved = jnp.pad(moved, ((0, 0), (0, 0), (0, 0), (0, 128 - 4 * share)))
         moved = jnp.concatenate([moved.reshape(devices, inputs, 256), codes], axis=2)
     moved = moved.reshape(devices * inputs, -1)
 
-    means = stack_means(moved, owner, padded, feeds)
+    means = stack_means(moved, place)
     means = means.reshape(feeds, padded, -1)
     landed = lax.all_to_all(means, "feed", split_axis=0, concat_axis=0, tiled=True)
     if direct:

time: 47.8 us -> 46.6 us (0.975)
  Pallas kernels: 17 us -> 16.1 us
    pallas_call x1 -> x2, Pallas kernels: 11.9 us -> 11.4 us  [the longest x1 11.2 us: stack_means(): pl.pallas_call(stack_kernel, out_shape=jax.ShapeDtypeStruct((place.shape[...]
  transfers between devices with their start and end apart: 1 -> 1, of which waited for: 1 -> 1; matrix products, arithmetic and copies ran while one was open for 0% -> 0% of each run, Pallas kernels for 0% -> 1%
where the time goes in v3:
time: 46.6 us; the launch traced here: 46.3 us
  Pallas kernels  16.1 us (35%)
  waiting for transfers between devices  11.9 us (26%)
  blocking collectives  10.9 us (23%)
  starting transfers between devices  7.3 us (16%)
    all_to_all x1, waiting for transfers between devices, per_device(): lax.all_to_all(local, everyone, split_axis=0, concat_axis=0, tiled=True)  11.9 us
    pallas_call x1, Pallas kernels, stack_means(): pl.pallas_call(stack_kernel, out_shape=jax.ShapeDtypeStruct((place.shape[...  11.2 us
    all_to_all x1, blocking collectives, per_device(): lax.all_to_all(means, 'feed', split_axis=0, concat_axis=0, tiled=True)  10.9 us
    all_to_all x1, starting transfers between devices, per_device(): lax.all_to_all(local, everyone, split_axis=0, concat_axis=0, tiled=True)  7.3 us
    pallas_call x1, Pallas kernels, channelize(): pl.pallas_call(functools.partial(channelize_kernel, direct), out_shape=ja...  3.73 us
  transfers between devices with their start and end apart: 1, of which 1 were waited for; matrix products, arithmetic and copies ran while one was open for 0% of the time, Pallas kernels for 1%

profile of v3, /device:TPU:0, one launch (start us, length us, event | category | flops | bytes accessed | tf_op | source)
XLA Modules:
  0.0 46.3 jit_solution(13377672661539524603)
XLA Ops:
  0.0 0.0 copy-start
  0.0 3.7 %channelize.1 = bf16[256,640]{1,0:T(8,128)(2,1)} custom-call(bf16[8,90112]{1,0:T(8,128)(2,1)} %x_hbm.1, s32[32,256]{1,0:T(8,128)} %code_hbm.1, f32[8,8192]{1,0:T(8,128)} %constant.12.clone.window_hbm, bf16[128,64]{1,0:T(8,128)(2,1)} %constant.13.clone.first_hbm, f32[64,128]{1,0:T(8,128)} %constant.14.clone.cos_hbm, f32[64,128]{1,0:T(8,128)} %constant.15.clone.sin_hbm, ...), custom_call_target="tpu_custom_call" | custom-call | tf_op jit(solution)/shard_map/channelize/pallas_call | solution.py:177
  3.7 7.3 %all-to-all-start = ((bf16[32,8,640]{2,1,0:T(8,128)(2,1)}), bf16[32,8,640]{2,1,0:T(8,128)(2,1)S(1)}, u32[]{:S(2)}, u32[]{:S(2)}) async-start(bf16[32,8,640]{2,1,0:T(8,128)(2,1)} %bitcast.12), calls=%async_computation | async-start | bytes 655360 | tf_op jit(solution)/shard_map/all_to_all | solution.py:468
  11.1 0.0 copy-done
  11.1 0.3 place_stacks.1.place_ref
  11.4 11.9 %all-to-all-done = bf16[32,8,640]{2,1,0:T(8,128)(2,1)S(1)} async-done(((bf16[32,8,640]{2,1,0:T(8,128)(2,1)}), bf16[32,8,640]{2,1,0:T(8,128)(2,1)S(1)}, u32[]{:S(2)}, u32[]{:S(2)}) %all-to-all-start) | async-done | bytes 327712 | tf_op jit(solution)/shard_map/all_to_all | solution.py:468
  23.3 11.2 %stack_means.1 = bf16[768,128]{1,0:T(8,128)(2,1)S(1)} custom-call(bf16[256,640]{1,0:T(8,128)(2,1)S(1)} %bitcast.9, bf16[768,384]{1,0:T(8,128)(2,1)S(1)} %place_stacks.1.place_ref), custom_call_target="tpu_custom_call" | custom-call | tf_op jit(solution)/shard_map/stack_means/pallas_call | solution.py:395
  34.5 10.9 %all_to_all.10 = bf16[8,96,128]{2,1,0:T(8,128)(2,1)S(1)} all-to-all(bf16[8,96,128]{2,1,0:T(8,128)(2,1)S(1)} %bitcast.11), channel_id=1, replica_groups=mesh['feed'=8,'chan'=4] {'feed'}, dimensions={0} | all-to-all | bytes 393216 | tf_op jit(solution)/shard_map/all_to_all | solution.py:478
  45.4 0.9 %lay_out.1 = f32[760,128]{1,0:T(8,128)} custom-call(bf16[768,128]{1,0:T(8,128)(2,1)S(1)} %bitcast.10), custom_call_target="tpu_custom_call" | custom-call | tf_op jit(solution)/shard_map/lay_out/pallas_call | solution.py:428
  (3 shorter events, 0.0 us)
Async XLA Ops:
  0.0 11.1 %copy-start = (s32[382]{0:T(512)S(1)}, s32[382]{0:T(512)}, u32[]{:S(2)}) copy-start(s32[382]{0:T(512)} %param.10) | copy-start | bytes 4588
  3.7 19.6 %all-to-all-start = ((bf16[32,8,640]{2,1,0:T(8,128)(2,1)}), bf16[32,8,640]{2,1,0:T(8,128)(2,1)S(1)}, u32[]{:S(2)}, u32[]{:S(2)}) async-start(bf16[32,8,640]{2,1,0:T(8,128)(2,1)} %bitcast.12), calls=%async_computation | async-start | bytes 655360 | tf_op jit(solution)/shard_map/all_to_all | solution.py:468

commit v4 on v3

--- a/solution.py
+++ b/solution.py
@@ -21,7 +21,6 @@
 HALF_STACKS = 192
 GROUP = 16
 PIECES = 2
-PARTS = (slice(0, GROUP),)
 CODE_BASE = 384
 MB = 1024 * 1024
 
@@ -214,7 +213,7 @@
 
 
 def stack_kernel(
-    data_ref, place_ref, out_ref, wide, pairs, other, twin, goal_ref, mask_ref, held, acc, tally
+    data_ref, place_ref, out_ref, wide, pairs, other, twin, goal_ref, mask_ref, held, acc
 ):
     inputs = data_ref.shape[0]
     half = inputs // 2
@@ -239,7 +238,10 @@
     col = lax.broadcasted_iota(jnp.int32, (half, inputs), 1)
     upper = target >= HALF_STACKS
     used = col != row
-    goal_ref[...] = jnp.where(upper, target - HALF_STACKS, target).astype(jnp.float32)
+    goal = jnp.where(upper, target - HALF_STACKS, target).astype(jnp.float32).T
+    for g in range(steps):
+        rolled = pltpu.roll(goal, (half - g * GROUP) % half, 1) if g else goal
+        goal_ref[g * inputs : (g + 1) * inputs, :] = rolled
     left = jnp.where(used & ~upper, 1.0, 0.0)
     right = jnp.where(used & upper, 1.0, 0.0)
     sign = jnp.where(code >= 0, 1.0, -1.0)
@@ -269,7 +271,6 @@
                     at = (b * 2 + part) * 256 + m * 128 + side * 64
                     twin[at : at + 64, side * half : (side + 1) * half] = other[source, half:]
     acc[...] = jnp.zeros(acc.shape, jnp.float32)
-    tally[...] = jnp.zeros(tally.shape, jnp.float32)
 
     def diagonal(rows):
         row = lax.broadcasted_iota(jnp.int32, (rows, 128), 0)
@@ -280,8 +281,10 @@
         return jnp.where(row == channel, 1.0, 0.0)
 
     diagonal_32, diagonal_16 = diagonal(32), diagonal(16)
-    stack = lax.broadcasted_iota(jnp.int32, (HALF_STACKS, inputs), 0)
+    stack = lax.broadcasted_iota(jnp.int32, (inputs, HALF_STACKS), 1)
     stack = stack.astype(jnp.float32).astype(jnp.bfloat16)
+    row = lax.broadcasted_iota(jnp.int32, (16, inputs), 0)
+    first_row, second_row = row == 0, row == 1
 
     def spread(reals, imags, mask):
         parts = []
@@ -292,12 +295,8 @@
             parts.append(jnp.concatenate([imag, -real], axis=1))
         return jnp.concatenate(parts, axis=0).astype(jnp.bfloat16)
 
-    def at_step(g, rows):
-        return g * rows if isinstance(g, int) else pl.multiple_of(g * rows, rows)
-
     def multiply(g):
-        start = at_step(g, GROUP)
-        start_pair = at_step(g, GROUP // 2)
+        start, start_pair = g * GROUP, g * GROUP // 2
         row = lax.broadcasted_iota(jnp.int32, (GROUP, half), 0) + start
         col = lax.broadcasted_iota(jnp.int32, (GROUP, half), 1)
         ahead = jnp.where(col > row, 1.0, 0.0)
@@ -337,50 +336,40 @@
                     held[at : at + 32, u * inputs : (u + 1) * inputs] = both.astype(jnp.bfloat16)
 
     def accumulate(g):
-        start = at_step(g, GROUP)
-        goal = goal_ref[pl.ds(start, GROUP), :].astype(jnp.bfloat16)
+        start = g * GROUP
+        goal = goal_ref[g * inputs : (g + 1) * inputs, :]
         masks = [mask_ref[n, pl.ds(start, GROUP), :].astype(jnp.bfloat16) for n in range(4)]
         members, values = [], []
-        lefts = rights = None
         for u in range(GROUP):
             columns = slice(u * inputs, (u + 1) * inputs)
             left, right, left_sign, right_sign = [mask[u : u + 1] for mask in masks]
             real = held[: width // 2, columns]
             imag = held[width // 2 :, columns]
+            tally = jnp.where(first_row, left, jnp.where(second_row, right, jnp.zeros_like(right)))
             values.append(
                 jnp.concatenate(
-                    [real * left, imag * left_sign, real * right, imag * right_sign], axis=0
+                    [real * left, imag * left_sign, real * right, imag * right_sign, tally], axis=0
                 )
             )
-            member = jnp.where(
-                stack == goal[u : u + 1], jnp.ones_like(stack), jnp.zeros_like(stack)
-            )
-            members.append(member)
-            lefts = member * left if lefts is None else lefts + member * left
-            rights = member * right if rights is None else rights + member * right
-        for n, part in enumerate(PARTS):
-            acc[n] += lax.dot_general(
-                jnp.concatenate(members[part], axis=1),
-                jnp.concatenate(values[part], axis=1),
-                (((1,), (1,)), ((), ())),
-                preferred_element_type=jnp.float32,
-            )
-        tally[0] += lefts.astype(jnp.float32)
-        tally[1] += rights.astype(jnp.float32)
-
-    def step(g, carry):
+            mine = jnp.broadcast_to(goal[:, u : u + 1], stack.shape).astype(jnp.bfloat16)
+            members.append(jnp.where(stack == mine, jnp.ones_like(stack), jnp.zeros_like(stack)))
+        acc[...] += jnp.dot(
+            jnp.concatenate(values, axis=1),
+            jnp.concatenate(members, axis=0),
+            preferred_element_type=jnp.float32,
+        )
+
+    multiply(0)
+    for g in range(steps - 1):
         accumulate(g)
         multiply(g + 1)
-        return carry
-
-    multiply(0)
-    lax.fori_loop(0, steps - 1, step, 0)
     accumulate(steps - 1)
 
+    totals = acc[...].T
     means = []
     for n in range(2):
-        counts = jnp.maximum(jnp.sum(tally[n], axis=1, keepdims=True), 1.0)
-        total = sum(acc[k, :, n * width : (n + 1) * width] for k in range(len(PARTS)))
+        counts = jnp.maximum(totals[:, 2 * width + n : 2 * width + n + 1], 1.0)
+        total = totals[:, n * width : (n + 1) * width]
         means.append((total / counts).astype(jnp.bfloat16))
     means = jnp.concatenate(means, axis=0)
     moved = jnp.dot(place_ref[...], means, preferred_element_type=jnp.float32)
@@ -400,11 +389,10 @@
             pltpu.VMEM((lanes // 128 * half, 128), jnp.float32),
             pltpu.VMEM((lanes, inputs), jnp.bfloat16),
             pltpu.VMEM((2 * lanes, inputs), jnp.bfloat16),
-            pltpu.VMEM((half, inputs), jnp.float32),
+            pltpu.VMEM((half // GROUP * inputs, half), jnp.float32),
             pltpu.VMEM((4, half, inputs), jnp.float32),
             pltpu.VMEM((width, GROUP * inputs), jnp.bfloat16),
-            pltpu.VMEM((len(PARTS), HALF_STACKS, 2 * width), jnp.float32),
-            pltpu.VMEM((2, HALF_STACKS, inputs), jnp.float32),
+            pltpu.VMEM((2 * width + 16, HALF_STACKS), jnp.float32),
         ],
         compiler_params=pltpu.CompilerParams(vmem_limit_bytes=48 * MB),
         name="stack_means",

time: 46.6 us -> 45.2 us (0.970)
  Pallas kernels: 16.1 us -> 14.7 us
    pallas_call x1, Pallas kernels: 11.2 us -> 9.76 us  [stack_means(): pl.pallas_call(stack_kernel, out_shape=jax.ShapeDtypeStruct((place.shape[...]
where the time goes in v4:
time: 45.2 us; the launch traced here: 45 us
  Pallas kernels  14.7 us (33%)
  waiting for transfers between devices  11.9 us (26%)
  blocking collectives  10.9 us (24%)
  starting transfers between devices  7.3 us (16%)
    all_to_all x1, waiting for transfers between devices, per_device(): lax.all_to_all(local, everyone, split_axis=0, concat_axis=0, tiled=True)  11.9 us
    all_to_all x1, blocking collectives, per_device(): lax.all_to_all(means, 'feed', split_axis=0, concat_axis=0, tiled=True)  10.9 us
    pallas_call x1, Pallas kernels, stack_means(): pl.pallas_call(stack_kernel, out_shape=jax.ShapeDtypeStruct((place.shape[...  9.76 us
    all_to_all x1, starting transfers between devices, per_device(): lax.all_to_all(local, everyone, split_axis=0, concat_axis=0, tiled=True)  7.3 us
    pallas_call x1, Pallas kernels, channelize(): pl.pallas_call(functools.partial(channelize_kernel, direct), out_shape=ja...  3.73 us
  transfers between devices with their start and end apart: 1, of which 1 were waited for; matrix products, arithmetic and copies ran while one was open for 0% of the time, Pallas kernels for 1%

profile of v4, /device:TPU:0, one launch (start us, length us, event | category | flops | bytes accessed | tf_op | source)
XLA Modules:
  0.0 45.0 jit_solution(16900470239275376281)
XLA Ops:
  0.0 0.0 copy-start
  0.0 3.7 %channelize.1 = bf16[256,640]{1,0:T(8,128)(2,1)} custom-call(bf16[8,90112]{1,0:T(8,128)(2,1)} %x_hbm.1, s32[32,256]{1,0:T(8,128)} %code_hbm.1, f32[8,8192]{1,0:T(8,128)} %constant.12.clone.window_hbm, bf16[128,64]{1,0:T(8,128)(2,1)} %constant.13.clone.first_hbm, f32[64,128]{1,0:T(8,128)} %constant.14.clone.cos_hbm, f32[64,128]{1,0:T(8,128)} %constant.15.clone.sin_hbm, ...), custom_call_target="tpu_custom_call" | custom-call | tf_op jit(solution)/shard_map/channelize/pallas_call | solution.py:176
  3.7 7.3 %all-to-all-start = ((bf16[32,8,640]{2,1,0:T(8,128)(2,1)}), bf16[32,8,640]{2,1,0:T(8,128)(2,1)S(1)}, u32[]{:S(2)}, u32[]{:S(2)}) async-start(bf16[32,8,640]{2,1,0:T(8,128)(2,1)} %bitcast.12), calls=%async_computation | async-start | bytes 655360 | tf_op jit(solution)/shard_map/all_to_all | solution.py:456
  11.1 0.0 copy-done
  11.1 0.3 place_stacks.1.place_ref
  11.4 11.9 %all-to-all-done = bf16[32,8,640]{2,1,0:T(8,128)(2,1)S(1)} async-done(((bf16[32,8,640]{2,1,0:T(8,128)(2,1)}), bf16[32,8,640]{2,1,0:T(8,128)(2,1)S(1)}, u32[]{:S(2)}, u32[]{:S(2)}) %all-to-all-start) | async-done | bytes 327712 | tf_op jit(solution)/shard_map/all_to_all | solution.py:456
  23.3 9.8 %stack_means.1 = bf16[768,128]{1,0:T(8,128)(2,1)S(1)} custom-call(bf16[256,640]{1,0:T(8,128)(2,1)S(1)} %bitcast.9, bf16[768,384]{1,0:T(8,128)(2,1)S(1)} %place_stacks.1.place_ref), custom_call_target="tpu_custom_call" | custom-call | tf_op jit(solution)/shard_map/stack_means/pallas_call | solution.py:384
  33.1 10.9 %all_to_all.10 = bf16[8,96,128]{2,1,0:T(8,128)(2,1)S(1)} all-to-all(bf16[8,96,128]{2,1,0:T(8,128)(2,1)S(1)} %bitcast.11), channel_id=1, replica_groups=mesh['feed'=8,'chan'=4] {'feed'}, dimensions={0} | all-to-all | bytes 393216 | tf_op jit(solution)/shard_map/all_to_all | solution.py:466
  44.1 0.9 %lay_out.1 = f32[760,128]{1,0:T(8,128)} custom-call(bf16[768,128]{1,0:T(8,128)(2,1)S(1)} %bitcast.10), custom_call_target="tpu_custom_call" | custom-call | tf_op jit(solution)/shard_map/lay_out/pallas_call | solution.py:416
  (3 shorter events, 0.0 us)
Async XLA Ops:
  0.0 11.1 %copy-start = (s32[382]{0:T(512)S(1)}, s32[382]{0:T(512)}, u32[]{:S(2)}) copy-start(s32[382]{0:T(512)} %param.10) | copy-start | bytes 4588
  3.7 19.6 %all-to-all-start = ((bf16[32,8,640]{2,1,0:T(8,128)(2,1)}), bf16[32,8,640]{2,1,0:T(8,128)(2,1)S(1)}, u32[]{:S(2)}, u32[]{:S(2)}) async-start(bf16[32,8,640]{2,1,0:T(8,128)(2,1)} %bitcast.12), calls=%async_computation | async-start | bytes 655360 | tf_op jit(solution)/shard_map/all_to_all | solution.py:456

commit v5 on v4

--- a/solution.py
+++ b/solution.py
@@ -19,7 +19,7 @@
 QS = CHANS // FA
 STACK_ROWS = 384
 HALF_STACKS = 192
-GROUP = 16
+GROUP = 32
 PIECES = 2
 CODE_BASE = 384
 MB = 1024 * 1024
@@ -199,30 +199,27 @@
     earlier = jnp.where((across == down) & (before < after), 1.0, 0.0)
     rank = jnp.sum(earlier, axis=0, keepdims=True)
     slot = jnp.where(owner >= 0, owner * padded, -STACK_ROWS) + rank
-    slot_id = lax.broadcasted_iota(jnp.int32, place_ref.shape, 0).astype(jnp.float32)
-    place_ref[...] = jnp.where(slot_id == slot, 1.0, 0.0).astype(jnp.bfloat16)
+    slot_id = lax.broadcasted_iota(jnp.int32, (place_ref.shape[0], STACK_ROWS), 0)
+    place = jnp.where(slot_id.astype(jnp.float32) == slot, 1.0, 0.0)
+    place_ref[...] = jnp.zeros(place_ref.shape, jnp.bfloat16)
+    for n in range(2):
+        half = place[:, n * HALF_STACKS : (n + 1) * HALF_STACKS].astype(jnp.bfloat16)
+        place_ref[:, n * 256 : n * 256 + HALF_STACKS] = half
 
 
 def place_stacks(owner, padded, feeds):
     return pl.pallas_call(
         functools.partial(place_kernel, padded),
-        out_shape=jax.ShapeDtypeStruct((feeds * padded, STACK_ROWS), jnp.bfloat16),
+        out_shape=jax.ShapeDtypeStruct((feeds * padded, 512), jnp.bfloat16),
         compiler_params=pltpu.CompilerParams(vmem_limit_bytes=16 * MB),
         name="place_stacks",
     )(owner)
 
 
-def stack_kernel(
-    data_ref, place_ref, out_ref, wide, pairs, other, twin, goal_ref, mask_ref, held, acc
-):
-    inputs = data_ref.shape[0]
+def decode(codes):
+    inputs = codes.shape[0]
     half = inputs // 2
-    lanes = data_ref.shape[1] - half
-    blocks = lanes // 256
-    width = lanes // SPECTRA
-    steps = half // GROUP
-
-    value = data_ref[:, lanes:].astype(jnp.float32).astype(jnp.int32)
+    value = codes.astype(jnp.float32).astype(jnp.int32)
     power = jnp.zeros(value.shape, jnp.int32)
     for e in range(1, 6):
         power = power + jnp.where(value >= 128 << e, 1, 0)
@@ -236,15 +233,27 @@
     target = jnp.where(code >= 0, code, -1 - code)
     row = lax.broadcasted_iota(jnp.int32, (half, inputs), 0)
     col = lax.broadcasted_iota(jnp.int32, (half, inputs), 1)
+    return target, col != row, jnp.where(code >= 0, 1.0, -1.0)
+
+
+def stack_kernel(
+    data_ref, place_ref, out_ref, wide, pairs, other, twin, goal_ref, mask_ref, held, acc
+):
+    inputs = data_ref.shape[0]
+    half = inputs // 2
+    lanes = data_ref.shape[1] - half
+    blocks = lanes // 256
+    width = lanes // SPECTRA
+    steps = half // GROUP
+
+    target, used, sign = decode(data_ref[:, lanes:])
     upper = target >= HALF_STACKS
-    used = col != row
     goal = jnp.where(upper, target - HALF_STACKS, target).astype(jnp.float32).T
     for g in range(steps):
         rolled = pltpu.roll(goal, (half - g * GROUP) % half, 1) if g else goal
         goal_ref[g * inputs : (g + 1) * inputs, :] = rolled
     left = jnp.where(used & ~upper, 1.0, 0.0)
     right = jnp.where(used & upper, 1.0, 0.0)
-    sign = jnp.where(code >= 0, 1.0, -1.0)
     for n, mask in enumerate((left, right, left * sign, right * sign)):
         mask_ref[n] = mask
 
@@ -365,15 +374,20 @@
         multiply(g + 1)
     accumulate(steps - 1)
 
-    totals = acc[...].T
     means = []
     for n in range(2):
-        counts = jnp.maximum(totals[:, 2 * width + n : 2 * width + n + 1], 1.0)
-        total = totals[:, n * width : (n + 1) * width]
-        means.append((total / counts).astype(jnp.bfloat16))
-    means = jnp.concatenate(means, axis=0)
-    moved = jnp.dot(place_ref[...], means, preferred_element_type=jnp.float32)
-    out_ref[...] = moved.astype(jnp.bfloat16)
+        counts = jnp.maximum(acc[2 * width + n : 2 * width + n + 1, :], 1.0)
+        means.append((acc[n * width : (n + 1) * width, :] / counts).astype(jnp.bfloat16))
+    moved = [
+        lax.dot_general(
+            place_ref[:, n * 256 : n * 256 + HALF_STACKS],
+            means[n],
+            (((1,), (1,)), ((), ())),
+            preferred_element_type=jnp.float32,
+        )
+        for n in range(2)
+    ]
+    out_ref[...] = (moved[0] + moved[1]).astype(jnp.bfloat16)
 
 
 def stack_means(data, place):
@@ -462,8 +476,9 @@
     moved = moved.reshape(devices * inputs, -1)
 
     means = stack_means(moved, place)
-    means = means.reshape(feeds, padded, -1)
-    landed = lax.all_to_all(means, "feed", split_axis=0, concat_axis=0, tiled=True)
+    landed = lax.all_to_all(
+        means.reshape(feeds, padded, -1), "feed", split_axis=0, concat_axis=0, tiled=True
+    )
     if direct:
         landed = lay_out(landed.reshape(feeds * padded, -1), feeds, padded, capacity)
         landed = landed.reshape(capacity, feeds // 2, 2, 128).transpose(0, 2, 1, 3)

time: 45.2 us -> 44.8 us (level)
  no operation moved by 1% of the time
where the time goes in v5:
time: 44.8 us; the launch traced here: 44.5 us
  Pallas kernels  14.3 us (32%)
  waiting for transfers between devices  11.9 us (27%)
  blocking collectives  10.9 us (24%)
  starting transfers between devices  7.3 us (16%)
    all_to_all x1, waiting for transfers between devices, per_device(): lax.all_to_all(local, everyone, split_axis=0, concat_axis=0, tiled=True)  11.9 us
    all_to_all x1, blocking collectives, per_device(): lax.all_to_all(means.reshape(feeds, padded, -1), 'feed', split_axis=0, co...  10.9 us
    pallas_call x1, Pallas kernels, stack_means(): pl.pallas_call(stack_kernel, out_shape=jax.ShapeDtypeStruct((place.shape[...  9.33 us
    all_to_all x1, starting transfers between devices, per_device(): lax.all_to_all(local, everyone, split_axis=0, concat_axis=0, tiled=True)  7.3 us
    pallas_call x1, Pallas kernels, channelize(): pl.pallas_call(functools.partial(channelize_kernel, direct), out_shape=ja...  3.73 us
    pallas_call x1, Pallas kernels, lay_out(): pl.pallas_call(functools.partial(lay_out_kernel, feeds, padded, capacity)...  0.9 us
  transfers between devices with their start and end apart: 1, of which 1 were waited for; matrix products, arithmetic and copies ran while one was open for 0% of the time, Pallas kernels for 1%

profile of v5, /device:TPU:0, one launch (start us, length us, event | category | flops | bytes accessed | tf_op | source)
XLA Modules:
  0.0 44.5 jit_solution(1928473683649023157)
XLA Ops:
  0.0 0.0 copy-start
  0.0 3.7 %channelize.1 = bf16[256,640]{1,0:T(8,128)(2,1)} custom-call(bf16[8,90112]{1,0:T(8,128)(2,1)} %x_hbm.1, s32[32,256]{1,0:T(8,128)} %code_hbm.1, f32[8,8192]{1,0:T(8,128)} %constant.12.clone.window_hbm, bf16[128,64]{1,0:T(8,128)(2,1)} %constant.13.clone.first_hbm, f32[64,128]{1,0:T(8,128)} %constant.14.clone.cos_hbm, f32[64,128]{1,0:T(8,128)} %constant.15.clone.sin_hbm, ...), custom_call_target="tpu_custom_call" | custom-call | tf_op jit(solution)/shard_map/channelize/pallas_call | solution.py:176
  3.7 7.3 %all-to-all-start = ((bf16[32,8,640]{2,1,0:T(8,128)(2,1)}), bf16[32,8,640]{2,1,0:T(8,128)(2,1)S(1)}, u32[]{:S(2)}, u32[]{:S(2)}) async-start(bf16[32,8,640]{2,1,0:T(8,128)(2,1)} %bitcast.12), calls=%async_computation | async-start | bytes 655360 | tf_op jit(solution)/shard_map/all_to_all | solution.py:470
  11.1 0.0 copy-done
  11.1 0.3 place_stacks.1.place_ref
  11.4 11.9 %all-to-all-done = bf16[32,8,640]{2,1,0:T(8,128)(2,1)S(1)} async-done(((bf16[32,8,640]{2,1,0:T(8,128)(2,1)}), bf16[32,8,640]{2,1,0:T(8,128)(2,1)S(1)}, u32[]{:S(2)}, u32[]{:S(2)}) %all-to-all-start) | async-done | bytes 327712 | tf_op jit(solution)/shard_map/all_to_all | solution.py:470
  23.3 9.3 %stack_means.1 = bf16[768,128]{1,0:T(8,128)(2,1)S(1)} custom-call(bf16[256,640]{1,0:T(8,128)(2,1)S(1)} %bitcast.9, bf16[768,512]{1,0:T(8,128)(2,1)S(1)} %place_stacks.1.place_ref), custom_call_target="tpu_custom_call" | custom-call | tf_op jit(solution)/shard_map/stack_means/pallas_call | solution.py:398
  32.7 10.9 %all_to_all.10 = bf16[8,96,128]{2,1,0:T(8,128)(2,1)S(1)} all-to-all(bf16[8,96,128]{2,1,0:T(8,128)(2,1)S(1)} %bitcast.10), channel_id=1, replica_groups=mesh['feed'=8,'chan'=4] {'feed'}, dimensions={0} | all-to-all | bytes 393216 | tf_op jit(solution)/shard_map/all_to_all | solution.py:479
  43.6 0.9 %lay_out.1 = f32[760,128]{1,0:T(8,128)} custom-call(bf16[768,128]{1,0:T(8,128)(2,1)S(1)} %bitcast.11), custom_call_target="tpu_custom_call" | custom-call | tf_op jit(solution)/shard_map/lay_out/pallas_call | solution.py:430
  (3 shorter events, 0.0 us)
Async XLA Ops:
  0.0 11.1 %copy-start = (s32[382]{0:T(512)S(1)}, s32[382]{0:T(512)}, u32[]{:S(2)}) copy-start(s32[382]{0:T(512)} %param.10) | copy-start | bytes 4588
  3.7 19.6 %all-to-all-start = ((bf16[32,8,640]{2,1,0:T(8,128)(2,1)}), bf16[32,8,640]{2,1,0:T(8,128)(2,1)S(1)}, u32[]{:S(2)}, u32[]{:S(2)}) async-start(bf16[32,8,640]{2,1,0:T(8,128)(2,1)} %bitcast.12), calls=%async_computation | async-start | bytes 655360 | tf_op jit(solution)/shard_map/all_to_all | solution.py:470

commit v6 on v5

--- a/solution.py
+++ b/solution.py
@@ -21,6 +21,7 @@
 HALF_STACKS = 192
 GROUP = 32
 PIECES = 2
+AHEAD = 2
 CODE_BASE = 384
 MB = 1024 * 1024
 
@@ -59,54 +60,60 @@
 
 
 def channelize_kernel(
-    direct, x_hbm, code_hbm, window_hbm, first_hbm, cos_hbm, sin_hbm, second_hbm, out_ref,
+    direct, x_hbm, code_hbm, window_hbm, first_hbm, cos_hbm, sin_hbm, second_hbm, out_hbm,
     x_ref, code_ref, window_ref, first_ref, cos_ref, sin_ref, second_ref, frames, mixed, turned,
-    x_sems, sems,
+    out_ref, x_sems, sems, out_sems,
 ):
     inputs = x_ref.shape[0]
     piece = FRAME // PIECES
-    pieces = []
-    for k in range(PIECES):
-        window_copy = pltpu.make_async_copy(
-            window_hbm.at[:, k * piece : (k + 1) * piece],
-            window_ref.at[:, k * piece : (k + 1) * piece],
-            x_sems.at[k, 0],
-        )
-        window_copy.start()
-        copies = [window_copy]
+    pieces = {}
+
+    def fetch(k):
+        at = slice(k * piece, (k + 1) * piece)
+        copies = [
+            pltpu.make_async_copy(window_hbm.at[:, at], window_ref.at[:, at], x_sems.at[k, 0])
+        ]
         for r in range(SPECTRA + TAPS - 1):
             at = slice(r * FRAME + k * piece, r * FRAME + (k + 1) * piece)
-            copy = pltpu.make_async_copy(x_hbm.at[:, at], x_ref.at[:, at], x_sems.at[k, 1 + r])
+            copies.append(
+                pltpu.make_async_copy(x_hbm.at[:, at], x_ref.at[:, at], x_sems.at[k, 1 + r])
+            )
+        for copy in copies:
             copy.start()
-            copies.append(copy)
-        pieces.append(copies)
-    others = []
-    for n, (source, target) in enumerate(
-        [
-            (code_hbm, code_ref),
-            (first_hbm, first_ref),
-            (cos_hbm, cos_ref),
-            (sin_hbm, sin_ref),
-            (second_hbm, second_ref),
-        ]
-    ):
-        copy = pltpu.make_async_copy(source, target, sems.at[n])
+        pieces[k] = copies
+
+    for k in range(min(AHEAD, PIECES)):
+        fetch(k)
+    others = [
+        pltpu.make_async_copy(source, target, sems.at[n])
+        for n, (source, target) in enumerate(
+            [
+                (code_hbm, code_ref),
+                (first_hbm, first_ref),
+                (cos_hbm, cos_ref),
+                (sin_hbm, sin_ref),
+                (second_hbm, second_ref),
+            ]
+        )
+    ]
+    for copy in others:
         copy.start()
-        others.append(copy)
-
-    for a in range(FA):
-        if a % (FA // PIECES) == 0:
-            for copy in pieces[a // (FA // PIECES)]:
-                copy.wait()
-        sums = [None] * SPECTRA
-        for r in range(SPECTRA + TAPS - 1):
-            x = x_ref[:, r * FRAME + a * FB : r * FRAME + (a + 1) * FB].astype(jnp.float32)
+
+    for k in range(PIECES):
+        for copy in pieces[k]:
+            copy.wait()
+        if k + AHEAD < PIECES:
+            fetch(k + AHEAD)
+        for a in range(k * FA // PIECES, (k + 1) * FA // PIECES):
+            sums = [None] * SPECTRA
+            for r in range(SPECTRA + TAPS - 1):
+                x = x_ref[:, r * FRAME + a * FB : r * FRAME + (a + 1) * FB].astype(jnp.float32)
+                for t in range(SPECTRA):
+                    if 0 <= r - t < TAPS:
+                        term = window_ref[r - t : r - t + 1, a * FB : (a + 1) * FB] * x
+                        sums[t] = term if sums[t] is None else sums[t] + term
             for t in range(SPECTRA):
-                if 0 <= r - t < TAPS:
-                    term = window_ref[r - t : r - t + 1, a * FB : (a + 1) * FB] * x
-                    sums[t] = term if sums[t] is None else sums[t] + term
-        for t in range(SPECTRA):
-            frames[(t * FA + a) * inputs : (t * FA + a + 1) * inputs, :] = sums[t]
+                frames[(t * FA + a) * inputs : (t * FA + a + 1) * inputs, :] = sums[t]
     for copy in others:
         copy.wait()
 
@@ -129,36 +136,57 @@
     code = code.astype(jnp.float32)
     out_ref[:, 512:] = jnp.concatenate([code] * QS, axis=0).astype(jnp.bfloat16)
 
+    def send(n, at):
+        copy = pltpu.make_async_copy(out_ref.at[:, at], out_hbm.at[:, at], out_sems.at[n])
+        copy.start()
+        return copy
+
+    sent = [send(2, slice(512, 512 + half))]
+
     for t in range(SPECTRA):
-        wide = [frames[pl.ds(t * FA * inputs + i, FA, stride=inputs), :] for i in range(inputs)]
-        wide = jnp.concatenate([part.astype(jnp.bfloat16) for part in wide], axis=1)
-        section = jnp.dot(first_ref[...], wide, preferred_element_type=jnp.float32)
-        for i in range(inputs):
-            real = section[:FA, i * FB : (i + 1) * FB]
-            imag = section[FA:, i * FB : (i + 1) * FB]
+        for pair in range(inputs // 2):
+            wide = [
+                frames[pl.ds(t * FA * inputs + i, FA, stride=inputs), :].astype(jnp.bfloat16)
+                for i in (2 * pair, 2 * pair + 1)
+            ]
+            section = jnp.dot(
+                first_ref[...],
+                jnp.concatenate(wide, axis=1),
+                preferred_element_type=jnp.float32,
+            )
             cosine, sine = cos_ref[...], sin_ref[...]
-            twisted = jnp.concatenate(
-                [real * cosine + imag * sine, imag * cosine - real * sine], axis=1
-            ).astype(jnp.bfloat16)
-            for part in range(4):
-                start = (i * 4 + part) * 64 + t * 16
-                mixed[start : start + 16, :] = twisted[part * 16 : (part + 1) * 16]
-    for i in range(inputs):
-        spectra = lax.dot_general(
-            second_ref[...],
-            mixed[i * 256 : (i + 1) * 256, :],
-            (((1,), (1,)), ((), ())),
-            preferred_element_type=jnp.float32,
-        ) * (1.0 / math.sqrt(FRAME))
-        for m in range(2):
-            for g in range(QS // 8):
-                for h in range(2):
-                    tile = spectra[m * QS + g * 8 : m * QS + g * 8 + 8, h * 128 : (h + 1) * 128]
-                    start = ((h * 2 + m) * QS + g * 8) * inputs + i
-                    turned[pl.ds(start, 8, stride=inputs), :] = tile
-    for part in range(4):
-        rows = turned[part * QS * inputs : (part + 1) * QS * inputs, :]
-        out_ref[:, part * 128 : (part + 1) * 128] = rows.astype(jnp.bfloat16)
+            for i in range(2):
+                real = section[:FA, i * FB : (i + 1) * FB]
+                imag = section[FA:, i * FB : (i + 1) * FB]
+                twisted = jnp.concatenate(
+                    [real * cosine + imag * sine, imag * cosine - real * sine], axis=1
+                ).astype(jnp.bfloat16)
+                for part in range(4):
+                    start = (part // 2 * inputs + 2 * pair + i) * 128 + part % 2 * 64 + t * 16
+                    mixed[start : start + 16, :] = twisted[part * 16 : (part + 1) * 16]
+    for h in range(2):
+        for pair in range(inputs // 2):
+            start = (h * inputs + 2 * pair) * 128
+            spectra = lax.dot_general(
+                second_ref[...],
+                mixed[start : start + 256, :],
+                (((1,), (1,)), ((), ())),
+                preferred_element_type=jnp.float32,
+            ) * (1.0 / math.sqrt(FRAME))
+            for i in range(2):
+                for m in range(2):
+                    for g in range(QS // 8):
+                        row = m * QS + g * 8
+                        start = ((h * 2 + m) * QS + g * 8) * inputs + 2 * pair + i
+                        turned[pl.ds(start, 8, stride=inputs), :] = spectra[
+                            row : row + 8, i * 128 : (i + 1) * 128
+                        ]
+        for part in (2 * h, 2 * h + 1):
+            rows = turned[part * QS * inputs : (part + 1) * QS * inputs, :]
+            out_ref[:, part * 128 : (part + 1) * 128] = rows.astype(jnp.bfloat16)
+        sent.append(send(h, slice(h * 256, h * 256 + 256)))
+    for copy in sent:
+        copy.wait()
 
 
 def channelize(samples, codes, order, direct):
@@ -177,13 +205,16 @@
         functools.partial(channelize_kernel, direct),
         out_shape=jax.ShapeDtypeStruct((QS * inputs, 512 + codes.shape[1] // 2), jnp.bfloat16),
         in_specs=[pl.BlockSpec(memory_space=pl.ANY)] * len(operands),
+        out_specs=pl.BlockSpec(memory_space=pl.ANY),
         scratch_shapes=[pltpu.VMEM(value.shape, value.dtype) for value in operands]
         + [
             pltpu.VMEM((SPECTRA * inputs * FA, FB), jnp.float32),
             pltpu.VMEM((SPECTRA * inputs * FA, 2 * FB), jnp.bfloat16),
             pltpu.VMEM((4 * QS * inputs, 128), jnp.float32),
+            pltpu.VMEM((QS * inputs, 512 + codes.shape[1] // 2), jnp.bfloat16),
             pltpu.SemaphoreType.DMA((PIECES, SPECTRA + TAPS)),
             pltpu.SemaphoreType.DMA((5,)),
+            pltpu.SemaphoreType.DMA((3,)),
         ],
         compiler_params=pltpu.CompilerParams(vmem_limit_bytes=56 * MB),
         name="channelize",

time: 44.8 us -> 44.7 us (level)
  no operation moved by 1% of the time
where the time goes in v6:
time: 44.7 us; the launch traced here: 44.5 us
  Pallas kernels  14.3 us (32%)
  waiting for transfers between devices  11.9 us (27%)
  blocking collectives  10.9 us (24%)
  starting transfers between devices  7.3 us (16%)
    all_to_all x1, waiting for transfers between devices, per_device(): lax.all_to_all(local, everyone, split_axis=0, concat_axis=0, tiled=True)  11.9 us
    all_to_all x1, blocking collectives, per_device(): lax.all_to_all(means.reshape(feeds, padded, -1), 'feed', split_axis=0, co...  10.9 us
    pallas_call x1, Pallas kernels, stack_means(): pl.pallas_call(stack_kernel, out_shape=jax.ShapeDtypeStruct((place.shape[...  9.33 us
    all_to_all x1, starting transfers between devices, per_device(): lax.all_to_all(local, everyone, split_axis=0, concat_axis=0, tiled=True)  7.3 us
    pallas_call x1, Pallas kernels, channelize(): pl.pallas_call(functools.partial(channelize_kernel, direct), out_shape=ja...  3.72 us
    pallas_call x1, Pallas kernels, lay_out(): pl.pallas_call(functools.partial(lay_out_kernel, feeds, padded, capacity)...  0.9 us
  transfers between devices with their start and end apart: 1, of which 1 were waited for; matrix products, arithmetic and copies ran while one was open for 0% of the time, Pallas kernels for 1%

profile of v6, /device:TPU:0, one launch (start us, length us, event | category | flops | bytes accessed | tf_op | source)
XLA Modules:
  0.0 44.5 jit_solution(565153966229782805)
XLA Ops:
  0.0 0.0 copy-start
  0.0 3.7 %channelize.1 = bf16[256,640]{1,0:T(8,128)(2,1)} custom-call(bf16[8,90112]{1,0:T(8,128)(2,1)} %x_hbm.1, s32[32,256]{1,0:T(8,128)} %code_hbm.1, f32[8,8192]{1,0:T(8,128)} %constant.12.clone.window_hbm, bf16[128,64]{1,0:T(8,128)(2,1)} %constant.13.clone.first_hbm, f32[64,128]{1,0:T(8,128)} %constant.14.clone.cos_hbm, f32[64,128]{1,0:T(8,128)} %constant.15.clone.sin_hbm, ...), custom_call_target="tpu_custom_call" | custom-call | tf_op jit(solution)/shard_map/channelize/pallas_call | solution.py:204
  3.7 7.3 %all-to-all-start = ((bf16[32,8,640]{2,1,0:T(8,128)(2,1)}), bf16[32,8,640]{2,1,0:T(8,128)(2,1)S(1)}, u32[]{:S(2)}, u32[]{:S(2)}) async-start(bf16[32,8,640]{2,1,0:T(8,128)(2,1)} %bitcast.12), calls=%async_computation | async-start | bytes 655360 | tf_op jit(solution)/shard_map/all_to_all | solution.py:501
  11.0 0.0 copy-done
  11.1 0.3 place_stacks.1.place_ref
  11.4 11.9 %all-to-all-done = bf16[32,8,640]{2,1,0:T(8,128)(2,1)S(1)} async-done(((bf16[32,8,640]{2,1,0:T(8,128)(2,1)}), bf16[32,8,640]{2,1,0:T(8,128)(2,1)S(1)}, u32[]{:S(2)}, u32[]{:S(2)}) %all-to-all-start) | async-done | bytes 327712 | tf_op jit(solution)/shard_map/all_to_all | solution.py:501
  23.3 9.3 %stack_means.1 = bf16[768,128]{1,0:T(8,128)(2,1)S(1)} custom-call(bf16[256,640]{1,0:T(8,128)(2,1)S(1)} %bitcast.9, bf16[768,512]{1,0:T(8,128)(2,1)S(1)} %place_stacks.1.place_ref), custom_call_target="tpu_custom_call" | custom-call | tf_op jit(solution)/shard_map/stack_means/pallas_call | solution.py:429
  32.7 10.9 %all_to_all.10 = bf16[8,96,128]{2,1,0:T(8,128)(2,1)S(1)} all-to-all(bf16[8,96,128]{2,1,0:T(8,128)(2,1)S(1)} %bitcast.10), channel_id=1, replica_groups=mesh['feed'=8,'chan'=4] {'feed'}, dimensions={0} | all-to-all | bytes 393216 | tf_op jit(solution)/shard_map/all_to_all | solution.py:510
  43.6 0.9 %lay_out.1 = f32[760,128]{1,0:T(8,128)} custom-call(bf16[768,128]{1,0:T(8,128)(2,1)S(1)} %bitcast.11), custom_call_target="tpu_custom_call" | custom-call | tf_op jit(solution)/shard_map/lay_out/pallas_call | solution.py:461
  (3 shorter events, 0.0 us)
Async XLA Ops:
  0.0 11.0 %copy-start = (s32[382]{0:T(512)S(1)}, s32[382]{0:T(512)}, u32[]{:S(2)}) copy-start(s32[382]{0:T(512)} %param.10) | copy-start | bytes 4588
  3.7 19.6 %all-to-all-start = ((bf16[32,8,640]{2,1,0:T(8,128)(2,1)}), bf16[32,8,640]{2,1,0:T(8,128)(2,1)S(1)}, u32[]{:S(2)}, u32[]{:S(2)}) async-start(bf16[32,8,640]{2,1,0:T(8,128)(2,1)} %bitcast.12), calls=%async_computation | async-start | bytes 655360 | tf_op jit(solution)/shard_map/all_to_all | solution.py:501

commit v7 on v5

--- a/solution.py
+++ b/solution.py
@@ -19,7 +19,7 @@
 QS = CHANS // FA
 STACK_ROWS = 384
 HALF_STACKS = 192
-GROUP = 32
+GROUP = 16
 PIECES = 2
 CODE_BASE = 384
 MB = 1024 * 1024
@@ -342,7 +342,7 @@
                     chosen = jnp.where(use, mine[:, :half], low)
                     both = jnp.concatenate([chosen, mine[:, half:]], axis=1)
                     at = (p * blocks + b) * 32
-                    held[at : at + 32, u * inputs : (u + 1) * inputs] = both.astype(jnp.bfloat16)
+                    held[g % 2, at : at + 32, u * inputs : (u + 1) * inputs] = both.astype(jnp.bfloat16)
 
     def accumulate(g):
         start = g * GROUP
@@ -352,8 +352,8 @@
         for u in range(GROUP):
             columns = slice(u * inputs, (u + 1) * inputs)
             left, right, left_sign, right_sign = [mask[u : u + 1] for mask in masks]
-            real = held[: width // 2, columns]
-            imag = held[width // 2 :, columns]
+            real = held[g % 2, : width // 2, columns]
+            imag = held[g % 2, width // 2 :, columns]
             tally = jnp.where(first_row, left, jnp.where(second_row, right, jnp.zeros_like(right)))
             values.append(
                 jnp.concatenate(
@@ -370,8 +370,8 @@
 
     multiply(0)
     for g in range(steps - 1):
+        multiply(g + 1)
         accumulate(g)
-        multiply(g + 1)
     accumulate(steps - 1)
 
     means = []
@@ -405,7 +405,7 @@
             pltpu.VMEM((2 * lanes, inputs), jnp.bfloat16),
             pltpu.VMEM((half // GROUP * inputs, half), jnp.float32),
             pltpu.VMEM((4, half, inputs), jnp.float32),
-            pltpu.VMEM((width, GROUP * inputs), jnp.bfloat16),
+            pltpu.VMEM((2, width, GROUP * inputs), jnp.bfloat16),
             pltpu.VMEM((2 * width + 16, HALF_STACKS), jnp.float32),
         ],
         compiler_params=pltpu.CompilerParams(vmem_limit_bytes=48 * MB),

time: 44.8 us -> 44.8 us (level)
  no operation moved by 1% of the time
where the time goes in v7:
time: 44.8 us; the launch traced here: 44.5 us
  Pallas kernels  14.3 us (32%)
  waiting for transfers between devices  11.9 us (27%)
  blocking collectives  10.9 us (24%)
  starting transfers between devices  7.3 us (16%)
    all_to_all x1, waiting for transfers between devices, per_device(): lax.all_to_all(local, everyone, split_axis=0, concat_axis=0, tiled=True)  11.9 us
    all_to_all x1, blocking collectives, per_device(): lax.all_to_all(means.reshape(feeds, padded, -1), 'feed', split_axis=0, co...  10.9 us
    pallas_call x1, Pallas kernels, stack_means(): pl.pallas_call(stack_kernel, out_shape=jax.ShapeDtypeStruct((place.shape[...  9.33 us
    all_to_all x1, starting transfers between devices, per_device(): lax.all_to_all(local, everyone, split_axis=0, concat_axis=0, tiled=True)  7.3 us
    pallas_call x1, Pallas kernels, channelize(): pl.pallas_call(functools.partial(channelize_kernel, direct), out_shape=ja...  3.73 us
    pallas_call x1, Pallas kernels, lay_out(): pl.pallas_call(functools.partial(lay_out_kernel, feeds, padded, capacity)...  0.9 us
  transfers between devices with their start and end apart: 1, of which 1 were waited for; matrix products, arithmetic and copies ran while one was open for 0% of the time, Pallas kernels for 1%

profile of v7, /device:TPU:0, one launch (start us, length us, event | category | flops | bytes accessed | tf_op | source)
XLA Modules:
  0.0 44.5 jit_solution(5840656781407208768)
XLA Ops:
  0.0 0.0 copy-start
  0.0 3.7 %channelize.1 = bf16[256,640]{1,0:T(8,128)(2,1)} custom-call(bf16[8,90112]{1,0:T(8,128)(2,1)} %x_hbm.1, s32[32,256]{1,0:T(8,128)} %code_hbm.1, f32[8,8192]{1,0:T(8,128)} %constant.12.clone.window_hbm, bf16[128,64]{1,0:T(8,128)(2,1)} %constant.13.clone.first_hbm, f32[64,128]{1,0:T(8,128)} %constant.14.clone.cos_hbm, f32[64,128]{1,0:T(8,128)} %constant.15.clone.sin_hbm, ...), custom_call_target="tpu_custom_call" | custom-call | tf_op jit(solution)/shard_map/channelize/pallas_call | solution.py:176
  3.7 7.3 %all-to-all-start = ((bf16[32,8,640]{2,1,0:T(8,128)(2,1)}), bf16[32,8,640]{2,1,0:T(8,128)(2,1)S(1)}, u32[]{:S(2)}, u32[]{:S(2)}) async-start(bf16[32,8,640]{2,1,0:T(8,128)(2,1)} %bitcast.12), calls=%async_computation | async-start | bytes 655360 | tf_op jit(solution)/shard_map/all_to_all | solution.py:470
  11.1 0.0 copy-done
  11.1 0.3 place_stacks.1.place_ref
  11.4 11.9 %all-to-all-done = bf16[32,8,640]{2,1,0:T(8,128)(2,1)S(1)} async-done(((bf16[32,8,640]{2,1,0:T(8,128)(2,1)}), bf16[32,8,640]{2,1,0:T(8,128)(2,1)S(1)}, u32[]{:S(2)}, u32[]{:S(2)}) %all-to-all-start) | async-done | bytes 327712 | tf_op jit(solution)/shard_map/all_to_all | solution.py:470
  23.3 9.3 %stack_means.1 = bf16[768,128]{1,0:T(8,128)(2,1)S(1)} custom-call(bf16[256,640]{1,0:T(8,128)(2,1)S(1)} %bitcast.9, bf16[768,512]{1,0:T(8,128)(2,1)S(1)} %place_stacks.1.place_ref), custom_call_target="tpu_custom_call" | custom-call | tf_op jit(solution)/shard_map/stack_means/pallas_call | solution.py:398
  32.7 10.9 %all_to_all.10 = bf16[8,96,128]{2,1,0:T(8,128)(2,1)S(1)} all-to-all(bf16[8,96,128]{2,1,0:T(8,128)(2,1)S(1)} %bitcast.10), channel_id=1, replica_groups=mesh['feed'=8,'chan'=4] {'feed'}, dimensions={0} | all-to-all | bytes 393216 | tf_op jit(solution)/shard_map/all_to_all | solution.py:479
  43.6 0.9 %lay_out.1 = f32[760,128]{1,0:T(8,128)} custom-call(bf16[768,128]{1,0:T(8,128)(2,1)S(1)} %bitcast.11), custom_call_target="tpu_custom_call" | custom-call | tf_op jit(solution)/shard_map/lay_out/pallas_call | solution.py:430
  (3 shorter events, 0.0 us)
Async XLA Ops:
  0.0 11.1 %copy-start = (s32[382]{0:T(512)S(1)}, s32[382]{0:T(512)}, u32[]{:S(2)}) copy-start(s32[382]{0:T(512)} %param.10) | copy-start | bytes 4588
  3.7 19.6 %all-to-all-start = ((bf16[32,8,640]{2,1,0:T(8,128)(2,1)}), bf16[32,8,640]{2,1,0:T(8,128)(2,1)S(1)}, u32[]{:S(2)}, u32[]{:S(2)}) async-start(bf16[32,8,640]{2,1,0:T(8,128)(2,1)} %bitcast.12), calls=%async_computation | async-start | bytes 655360 | tf_op jit(solution)/shard_map/all_to_all | solution.py:470
